TPU v7x, 256 devices: a whole 4x4x8 slice. The times are simulated.
256 devices in a mesh: section: 32 (over z_hi, y, core), fsdp: 8 (over z_lo, x).
Axes of the slice: x: 4, y: 4, z: 8 (z_hi: 4, z_lo: 2; z = z_hi * 2 + z_lo), core: 2. Of those that a mesh axis runs over, the one named last changes fastest.
Arguments:
- handoff: bfloat16 [32, 8192, 640], P('section', 'fsdp'), may hold values from -6 to 6
- returning: bfloat16 [32, 8192, 640], P('section', 'fsdp'), may hold values from -6 to 6
- stashed_input: bfloat16 [32, 8192, 640], P('section', 'fsdp'), may hold values from -6 to 6
- skip_held: bfloat16 [32, 8192, 640], P('section', 'fsdp'), may hold values from -6 to 6
- timesteps_forward: int32 [32, 8], P('section', 'fsdp'), may hold values from 0 to 999
- timesteps_backward: int32 [32, 8], P('section', 'fsdp'), may hold values from 0 to 999
- section_level: int32 [32], P('section'), may hold values from 0 to 3
- level_embed: float32 [4, 256], replicated, may hold values from -6 to 6
- temporal_weight: bfloat16 [32, 1920, 640], P('section', 'fsdp'), may hold values from -0.125 to 0.125
- point_weight: bfloat16 [32, 640, 640], P('section', 'fsdp'), may hold values from -0.25 to 0.25
- film_weight: bfloat16 [32, 256, 1280], P('section', 'fsdp'), may hold values from -0.375 to 0.375
Outputs:
- handoff_next: bfloat16 [32, 8192, 640], P('section', 'fsdp')
- returning_next: bfloat16 [32, 8192, 640], P('section', 'fsdp')
- skip_next: bfloat16 [32, 8192, 640], P('section', 'fsdp')
- temporal_grad: float32 [32, 1920, 640], P('section', 'fsdp')
- pointwise_grad: float32 [32, 640, 640], P('section', 'fsdp')
- film_grad: float32 [32, 256, 1280], P('section', 'fsdp')
All inputs are finite; a program needn't handle non-finite values.
Results may differ from a plain program's by a relative error of at most 0.025.
Values may be sent and summed in bfloat16 or wider, within the bound.
A program may use at most 128 MiB of HBM per device.

v0:
```python
import math

import jax
import jax.numpy as jnp
from jax import lax
from jax.sharding import PartitionSpec as P

CHANNELS = 640
EMBED = 256
FRAMES = 16
LEVELS = 4


def passed_along(x, axis, by):
    length = lax.axis_size(axis)
    return lax.ppermute(x, axis, [(i, (i + by) % length) for i in range(length)])


def swapped(block, axis, stride):
    count = lax.axis_size(axis)
    route = []
    for low in range(count):
        high = low | 1 << stride
        if high != low and high < count:
            route += [(low, high), (high, low)]
    return lax.ppermute(block, axis, route)


def lookup_level(level_embed, level_index):
    onehot = (jnp.arange(LEVELS, dtype=jnp.int32) == level_index).astype(jnp.float32)
    return jnp.sum(onehot[:, None] * level_embed, axis=0)


def time_hidden(timesteps, level_row):
    half_width = EMBED // 2
    frequency = jnp.exp(-math.log(10000.0) * jnp.arange(half_width, dtype=jnp.float32) / half_width)
    phases = timesteps.astype(jnp.float32)[:, None] * frequency[None, :]
    embedded = jnp.concatenate([jnp.sin(phases), jnp.cos(phases)], axis=-1) + level_row[None, :]
    return jax.nn.silu(embedded).astype(jnp.bfloat16)


def unet_block(block_input, hidden, temporal_weight, point_weight, film_weight):
    sample_count = hidden.shape[0]
    film = jnp.dot(hidden, film_weight, preferred_element_type=jnp.float32)
    film_scale = film[:, :CHANNELS][:, None, None, :]
    film_shift = film[:, CHANNELS:][:, None, None, :]
    grid = block_input.reshape(sample_count, FRAMES, -1, CHANNELS)
    mean_square = jnp.mean(grid * grid, axis=-1, keepdims=True)
    normalized = grid * lax.rsqrt(mean_square + 1e-06)
    modulated = (normalized * (1.0 + film_scale) + film_shift).astype(jnp.bfloat16)
    blank = jnp.zeros_like(modulated[:, :1])
    earlier = jnp.concatenate([blank, modulated[:, :-1]], axis=1)
    later_frame = jnp.concatenate([modulated[:, 1:], blank], axis=1)
    stacked = jnp.concatenate([earlier, modulated, later_frame], axis=-1).reshape(-1, 3 * CHANNELS)
    temporal = jnp.dot(stacked, temporal_weight, preferred_element_type=jnp.float32)
    gated = jax.nn.silu(temporal).astype(jnp.bfloat16)
    return block_input + jnp.dot(gated, point_weight, preferred_element_type=jnp.float32)


def body(
    handoff,
    returning,
    stashed_input,
    skip_held,
    timesteps_forward,
    timesteps_backward,
    section_level,
    level_embed,
    temporal_weight,
    point_weight,
    film_weight,
):
    sections = lax.axis_size("section")
    midpoint = sections // 2
    bit_total = sections.bit_length() - 1
    encoder_side = lax.axis_index("section") < midpoint
    full_temporal, full_point, full_film = (
        lax.all_gather(temporal_weight, "fsdp", axis=1, tiled=True),
        lax.all_gather(point_weight, "fsdp", axis=1, tiled=True),
        lax.all_gather(film_weight, "fsdp", axis=1, tiled=True),
    )
    full_temporal, full_point, full_film = (full_temporal[0], full_point[0], full_film[0])
    arrived = passed_along(handoff, "section", 1)[0].astype(jnp.float32)
    going_back = passed_along(returning, "section", -1)[0].astype(jnp.float32)
    held_rows = skip_held[0].astype(jnp.float32)
    level_row = lookup_level(level_embed, section_level[0])
    hidden_forward = time_hidden(timesteps_forward[0], level_row)
    hidden_backward = time_hidden(timesteps_backward[0], level_row)
    stash_rows = stashed_input[0].astype(jnp.float32)
    zero_rows = jnp.zeros(handoff.shape[1:], jnp.bfloat16)

    def backward(output_grad):

        def local_block(first, second, third, fourth):
            return unet_block(first, hidden_backward, second, third, fourth)

        unused, pullback = jax.vjp(local_block, stash_rows, full_temporal, full_point, full_film)
        input_grad, grad_one, grad_two, grad_three = pullback(output_grad)
        return (
            input_grad.astype(jnp.bfloat16),
            (
                grad_one.astype(jnp.float32),
                grad_two.astype(jnp.float32),
                grad_three.astype(jnp.float32),
            ),
        )

    forward_input = arrived + jnp.where(encoder_side, 0.0, held_rows)
    backward_grad = going_back + jnp.where(encoder_side, held_rows, 0.0)
    section_out = unet_block(
        forward_input, hidden_forward, full_temporal, full_point, full_film
    ).astype(jnp.bfloat16)
    sent_rows = jnp.where(encoder_side, section_out, zero_rows)
    for bit_number in range(bit_total):
        sent_rows = swapped(sent_rows, "section", bit_number)
    input_grad, weight_grads = backward(backward_grad)
    sent_grad = jnp.where(encoder_side, zero_rows, input_grad)
    for bit_number in range(bit_total):
        sent_grad = swapped(sent_grad, "section", bit_number)
    skip_next = jnp.where(encoder_side, sent_grad, sent_rows)
    temporal_grad, pointwise_grad, film_grad = (
        lax.psum_scatter(
            weight_grads[0][None].astype(jnp.bfloat16), "fsdp", scatter_dimension=1, tiled=True
        ).astype(jnp.float32),
        lax.psum_scatter(
            weight_grads[1][None].astype(jnp.bfloat16), "fsdp", scatter_dimension=1, tiled=True
        ).astype(jnp.float32),
        lax.psum_scatter(
            weight_grads[2][None].astype(jnp.bfloat16), "fsdp", scatter_dimension=1, tiled=True
        ).astype(jnp.float32),
    )
    return (
        section_out[None],
        input_grad[None],
        skip_next[None],
        temporal_grad,
        pointwise_grad,
        film_grad,
    )


def solution(mesh):
    in_specs = (
        P("section", "fsdp", None),
        P("section", "fsdp", None),
        P("section", "fsdp", None),
        P("section", "fsdp", None),
        P("section", "fsdp"),
        P("section", "fsdp"),
        P("section"),
        P(),
        P("section", "fsdp", None),
        P("section", "fsdp", None),
        P("section", "fsdp", None),
    )
    out_specs = (
        P("section", "fsdp", None),
        P("section", "fsdp", None),
        P("section", "fsdp", None),
        P("section", "fsdp", None),
        P("section", "fsdp", None),
        P("section", "fsdp", None),
    )
    return jax.shard_map(body, mesh=mesh, in_specs=in_specs, out_specs=out_specs, check_vma=False)
```

profile of v0, /device:TPU:30, one launch (start us, length us, event | category | flops | bytes accessed | tf_op | source)
XLA Modules:
  0.0 561.2 jit_solution(4310325809907599972)
XLA Ops:
  7.2 0.7 all-gather.2.cloned.1.call-update
  8.1 1.7 collective-permute-start.1
  11.9 0.8 multiply_reduce_fusion.2
  12.7 1.6 multiply_reduce_fusion
  14.4 38.2 %all_gather.9 = bf16[1,256,1280]{2,1,0:T(8,128)(2,1)S(1)} all-gather(bf16[1,32,1280]{2,1,0:T(8,128)(2,1)} %param.21), channel_id=1, replica_groups=mesh['section'=32,'fsdp'=8] {'fsdp'}, dimensions={1}, use_global_device_ids=true | all-gather | bytes 737280 | tf_op jit(solution)/shard_map/all_gather | solution.py:80
  52.9 0.5 add_convert_fusion
  53.3 0.3 fusion.91
  53.7 1.3 concatenate.48
  55.0 1.2 concatenate.50
  56.4 1.5 fusion.19
  57.9 32.5 %all_gather.11 = bf16[1,640,640]{2,1,0:T(8,128)(2,1)} all-gather(bf16[1,80,640]{2,1,0:T(8,128)(2,1)S(1)} %copy-done.12), channel_id=1, replica_groups=mesh['section'=32,'fsdp'=8] {'fsdp'}, dimensions={1}, use_global_device_ids=true | all-gather | bytes 921600 | tf_op jit(solution)/shard_map/all_gather | solution.py:79
  90.5 6.0 %fusion.29 = f32[1024,640]{1,0:T(8,128)S(1)} fusion(bf16[1,1920,640]{2,1,0:T(8,128)(2,1)} %all-gather.2.cloned.1.call-done, bf16[1024,640]{1,0:T(8,128)(2,1)} %bitcast.103, bf16[1024,640]{1,0:T(8,128)(2,1)} %fusion.19, bf16[1024,640]{1,0:T(8,128)(2,1)} %bitcast.101), kind=kOutput, calls=%fused_computation.53 | convolution fusion | flops 2528378880 | bytes 9011200 | tf_op jit(solution)/shard_map/jvp()/dot_general | solution.py:55
  96.5 1.5 copy-done.14
  98.0 1.6 fusion.12
  99.6 3.6 convolution_convert_fusion
  103.2 0.4 fusion.90
  103.5 1.7 fusion.14
  105.3 1.0 fusion.62
  106.5 0.6 add_add_fusion
  107.2 1.6 copy-done.1
  108.8 3.3 multiply_reduce_fusion.1
  112.2 1.5 fusion.26
  113.7 0.4 add_convert_fusion.1
  114.1 0.3 fusion.92
  114.4 1.3 concatenate.42
  115.7 1.2 concatenate.44
  116.9 10.3 %broadcast_select_fusion = (bf16[1024,640]{1,0:T(8,128)(2,1)}, bf16[1024,640]{1,0:T(8,128)(2,1)}) fusion(pred[]{:T(512)S(6)} %lt.3, bf16[1,640,640]{2,1,0:T(8,128)(2,1)S(1)} %copy-done.11, bf16[1,1920,640]{2,1,0:T(8,128)(2,1)} %all-gather.2.cloned.1.call-done, bf16[1024,640]{1,0:T(8,128)(2,1)} %bitcast.106, bf16[1024,640]{1,0:T(8,128)(2,1)} %fusion.26, ...), kind=kOutput, calls=%fused_computation.66 | convolution fusion | flops 3372482560 | bytes 12451841 | tf_op jit(solution)/shard_map/dot_general | solution.py:57
  127.2 17.2 %collective-permute-start.7 = (bf16[1024,640]{1,0:T(8,128)(2,1)}, bf16[1024,640]{1,0:T(8,128)(2,1)}, u32[]{:S(2)}, u32[]{:S(2)}) collective-permute-start(bf16[1024,640]{1,0:T(8,128)(2,1)} %get-tuple-element.28), channel_id=1, source_target_pairs={{0,8},{8,0},{16,24},{24,16},{32,40},{40,32},{48,56},{56,48},{64,72... | collective-permute-start | bytes 3932168 | tf_op jit(solution)/shard_map/ppermute | solution.py:26
  144.4 4.2 fusion.40
  148.7 2.4 fusion.47
  151.4 0.6 collective-permute-done.2
  152.0 1.4 collective-permute-start.3
  153.4 6.4 %fusion.8 = bf16[1,1920,640]{2,1,0:T(8,128)(2,1)} fusion(bf16[1024,640]{1,0:T(8,128)(2,1)} %copy-done.16, bf16[1024,640]{1,0:T(8,128)(2,1)} %bitcast.104, bf16[1024,640]{1,0:T(8,128)(2,1)S(1)} %copy-done.8, bf16[1024,640]{1,0:T(8,128)(2,1)S(1)} %bitcast.102), kind=kOutput, calls=%fused_computation.20 | convolution fusion | flops 2528378880 | bytes 7700480 | tf_op jit(solution)/shard_map/transpose(jvp())/dot_general | solution.py:55
  159.8 23.4 %collective-permute-done.8 = bf16[1024,640]{1,0:T(8,128)(2,1)} collective-permute-done((bf16[1024,640]{1,0:T(8,128)(2,1)}, bf16[1024,640]{1,0:T(8,128)(2,1)}, u32[]{:S(2)}, u32[]{:S(2)}) %collective-permute-start.8) | collective-permute-done | bytes 1310752 | tf_op jit(solution)/shard_map/ppermute | solution.py:26
  183.3 23.5 %collective-permute-start.9 = (bf16[1024,640]{1,0:T(8,128)(2,1)}, bf16[1024,640]{1,0:T(8,128)(2,1)S(1)}, u32[]{:S(2)}, u32[]{:S(2)}) collective-permute-start(bf16[1024,640]{1,0:T(8,128)(2,1)} %collective-permute-done.8), channel_id=1, source_target_pairs={{0,32},{32,0},{8,40},{40,8},{16,48},{48,16},{24,56},{56,24},{64,96... | collective-permute-start | bytes 3932168 | tf_op jit(solution)/shard_map/ppermute | solution.py:26
  206.7 4.6 collective-permute-done.3
  211.4 23.5 %collective-permute-start.4 = (bf16[1024,640]{1,0:T(8,128)(2,1)}, bf16[1024,640]{1,0:T(8,128)(2,1)S(1)}, u32[]{:S(2)}, u32[]{:S(2)}) collective-permute-start(bf16[1024,640]{1,0:T(8,128)(2,1)} %collective-permute-done.3), channel_id=1, source_target_pairs={{0,32},{32,0},{8,40},{40,8},{16,48},{48,16},{24,56},{56,24},{64,96... | collective-permute-start | bytes 3932168 | tf_op jit(solution)/shard_map/ppermute | solution.py:26
  234.8 28.0 %collective-permute-done.9 = bf16[1024,640]{1,0:T(8,128)(2,1)S(1)} collective-permute-done((bf16[1024,640]{1,0:T(8,128)(2,1)}, bf16[1024,640]{1,0:T(8,128)(2,1)S(1)}, u32[]{:S(2)}, u32[]{:S(2)}) %collective-permute-start.9) | collective-permute-done | bytes 1310752 | tf_op jit(solution)/shard_map/ppermute | solution.py:26
  262.8 27.3 %collective-permute-done.4 = bf16[1024,640]{1,0:T(8,128)(2,1)S(1)} collective-permute-done((bf16[1024,640]{1,0:T(8,128)(2,1)}, bf16[1024,640]{1,0:T(8,128)(2,1)S(1)}, u32[]{:S(2)}, u32[]{:S(2)}) %collective-permute-start.4) | collective-permute-done | bytes 1310752 | tf_op jit(solution)/shard_map/ppermute | solution.py:26
  290.1 61.3 %collective-permute-done.10 = bf16[1024,640]{1,0:T(8,128)(2,1)} collective-permute-done((bf16[1024,640]{1,0:T(8,128)(2,1)S(1)}, bf16[1024,640]{1,0:T(8,128)(2,1)}, u32[]{:S(2)}, u32[]{:S(2)}) %collective-permute-start.10) | collective-permute-done | bytes 1310752 | tf_op jit(solution)/shard_map/ppermute | solution.py:26
  351.4 35.3 %collective-permute-start.11 = (bf16[1024,640]{1,0:T(8,128)(2,1)}, bf16[1024,640]{1,0:T(8,128)(2,1)S(1)}, u32[]{:S(2)}, u32[]{:S(2)}) collective-permute-start(bf16[1024,640]{1,0:T(8,128)(2,1)} %collective-permute-done.10), channel_id=1, source_target_pairs={{0,128},{128,0},{8,136},{136,8},{16,144},{144,16},{24,152},{152,24... | collective-permute-start | bytes 3932168 | tf_op jit(solution)/shard_map/ppermute | solution.py:26
  386.7 19.1 %collective-permute-done.5 = bf16[1024,640]{1,0:T(8,128)(2,1)} collective-permute-done((bf16[1024,640]{1,0:T(8,128)(2,1)S(1)}, bf16[1024,640]{1,0:T(8,128)(2,1)}, u32[]{:S(2)}, u32[]{:S(2)}) %collective-permute-start.5) | collective-permute-done | bytes 1310752 | tf_op jit(solution)/shard_map/ppermute | solution.py:26
  405.9 91.5 %collective-permute-start.6 = (bf16[1024,640]{1,0:T(8,128)(2,1)}, bf16[1024,640]{1,0:T(8,128)(2,1)S(1)}, u32[]{:S(2)}, u32[]{:S(2)}) collective-permute-start(bf16[1024,640]{1,0:T(8,128)(2,1)} %collective-permute-done.5), channel_id=1, source_target_pairs={{0,128},{128,0},{8,136},{136,8},{16,144},{144,16},{24,152},{152,24... | collective-permute-start | bytes 3932168 | tf_op jit(solution)/shard_map/ppermute | solution.py:26
  497.4 1.6 convert_element_type.230
  498.9 1.6 convert_element_type.227
  500.5 1.8 convert_element_type.223
  502.3 51.1 %collective-permute-done.6 = bf16[1024,640]{1,0:T(8,128)(2,1)S(1)} collective-permute-done((bf16[1024,640]{1,0:T(8,128)(2,1)}, bf16[1024,640]{1,0:T(8,128)(2,1)S(1)}, u32[]{:S(2)}, u32[]{:S(2)}) %collective-permute-start.6) | collective-permute-done | bytes 1310752 | tf_op jit(solution)/shard_map/ppermute | solution.py:26
  553.5 1.2 select_bitcast_fusion
  (71 shorter events, 1.6 us)
Async XLA Ops:
  7.2 45.7 %copy-start = (bf16[1,1024,640]{2,1,0:T(8,128)(2,1)S(1)}, bf16[1,1024,640]{2,1,0:T(8,128)(2,1)}, u32[]{:S(2)}) copy-start(bf16[1,1024,640]{2,1,0:T(8,128)(2,1)} %param.13) | copy-start | bytes 3932164
  7.2 83.3 %all-gather.2.cloned.1.call-start = ((), (), s32[]{:S(2)}) async-start(), calls=%async_computation.3 | async-start | bytes 2764800 | tf_op jit(solution)/shard_map/all_gather | solution.py:78
  7.9 489.4 %reduce-scatter.8.cloned.1.call-start = ((), (), s32[]{:S(2)}) async-start(), calls=%async_computation.6 | async-start | bytes 737280 | tf_op jit(solution)/shard_map/reduce_scatter | solution.py:128
  8.0 99.2 %collective-permute-start = (bf16[1,1024,640]{2,1,0:T(8,128)(2,1)}, bf16[1,1024,640]{2,1,0:T(8,128)(2,1)}, u32[]{:S(2)}, u32[]{:S(2)}) collective-permute-start(bf16[1,1024,640]{2,1,0:T(8,128)(2,1)} %param.11), channel_id=1, source_target_pairs={{0,8},{8,16},{16,24},{24,32},{32,40},{40,48},{48,56},{56,64},{64,7... | collective-permute-start | bytes 3932168 | tf_op jit(solution)/shard_map/ppermute | solution.py:16
  8.1 88.4 %collective-permute-start.1 = (bf16[1,1024,640]{2,1,0:T(8,128)(2,1)}, bf16[1,1024,640]{2,1,0:T(8,128)(2,1)S(1)}, u32[]{:S(2)}, u32[]{:S(2)}) collective-permute-start(bf16[1,1024,640]{2,1,0:T(8,128)(2,1)} %param.12), channel_id=1, source_target_pairs={{0,248},{8,0},{16,8},{24,16},{32,24},{40,32},{48,40},{56,48},{64,5... | collective-permute-start | bytes 3932168 | tf_op jit(solution)/shard_map/ppermute | solution.py:16
  54.9 3.0 copy-start.12
  90.5 7.5 %copy-start.2 = (bf16[1,1024,640]{2,1,0:T(8,128)(2,1)S(1)}, bf16[1,1024,640]{2,1,0:T(8,128)(2,1)}, u32[]{:S(2)}) copy-start(bf16[1,1024,640]{2,1,0:T(8,128)(2,1)} %param.14) | copy-start | bytes 3932164
  90.5 7.5 %copy-start.10 = (bf16[1,640,640]{2,1,0:T(8,128)(2,1)S(1)}, bf16[1,640,640]{2,1,0:T(8,128)(2,1)}, u32[]{:S(2)}) copy-start(bf16[1,640,640]{2,1,0:T(8,128)(2,1)} %all_gather.11) | copy-start | bytes 2457604
  96.5 1.5 copy-start.14
  96.5 3.1 copy-start.13
  98.0 1.6 copy-start.5
  99.6 3.6 copy-start.16
  106.3 392.6 %reduce-scatter.6.cloned.1.call-start = ((), (), s32[]{:S(2)}) async-start(), calls=%async_computation.5 | async-start | bytes 921600 | tf_op jit(solution)/shard_map/reduce_scatter | solution.py:125
  106.5 2.3 copy-start.3
  106.5 2.3 copy-start.6
  107.2 1.6 copy-start.1
  114.4 2.5 copy-start.11
  127.2 21.6 %copy-start.4 = (bf16[1,1024,640]{2,1,0:T(8,128)(2,1)S(1)}, bf16[1,1024,640]{2,1,0:T(8,128)(2,1)}, u32[]{:S(2)}) copy-start(bf16[1,1024,640]{2,1,0:T(8,128)(2,1)} %param.14) | copy-start | bytes 3932164
  127.2 21.6 %copy-start.7 = (bf16[1,1024,640]{2,1,0:T(8,128)(2,1)S(1)}, bf16[1,1024,640]{2,1,0:T(8,128)(2,1)}, u32[]{:S(2)}) copy-start(bf16[1,1024,640]{2,1,0:T(8,128)(2,1)} %copy-done.5) | copy-start | bytes 3932164
  127.2 21.6 %copy-start.15 = (f32[1024,640]{1,0:T(8,128)S(1)}, f32[1024,640]{1,0:T(8,128)}, u32[]{:S(2)}) copy-start(f32[1024,640]{1,0:T(8,128)} %copy-done.14) | copy-start | bytes 7864324
  127.2 24.1 %collective-permute-start.7 = (bf16[1024,640]{1,0:T(8,128)(2,1)}, bf16[1024,640]{1,0:T(8,128)(2,1)}, u32[]{:S(2)}, u32[]{:S(2)}) collective-permute-start(bf16[1024,640]{1,0:T(8,128)(2,1)} %get-tuple-element.28), channel_id=1, source_target_pairs={{0,8},{8,0},{16,24},{24,16},{32,40},{40,32},{48,56},{56,48},{64,72... | collective-permute-start | bytes 3932168 | tf_op jit(solution)/shard_map/ppermute | solution.py:26
  148.6 4.8 copy-start.8
  148.6 4.8 copy-start.9
  148.6 3.4 collective-permute-start.2
  151.2 349.3 %reduce-scatter.4.cloned.1.call-start = ((), (), s32[]{:S(2)}) async-start(), calls=%async_computation.4 | async-start | bytes 2764800 | tf_op jit(solution)/shard_map/reduce_scatter | solution.py:122
  151.3 32.0 %collective-permute-start.8 = (bf16[1024,640]{1,0:T(8,128)(2,1)}, bf16[1024,640]{1,0:T(8,128)(2,1)}, u32[]{:S(2)}, u32[]{:S(2)}) collective-permute-start(bf16[1024,640]{1,0:T(8,128)(2,1)} %collective-permute-done.7), channel_id=1, source_target_pairs={{0,16},{16,0},{8,24},{24,8},{32,48},{48,32},{40,56},{56,40},{64,80... | collective-permute-start | bytes 3932168 | tf_op jit(solution)/shard_map/ppermute | solution.py:26
  152.0 59.4 %collective-permute-start.3 = (bf16[1024,640]{1,0:T(8,128)(2,1)}, bf16[1024,640]{1,0:T(8,128)(2,1)}, u32[]{:S(2)}, u32[]{:S(2)}) collective-permute-start(bf16[1024,640]{1,0:T(8,128)(2,1)} %collective-permute-done.2), channel_id=1, source_target_pairs={{0,16},{16,0},{8,24},{24,8},{32,48},{48,32},{40,56},{56,40},{64,80... | collective-permute-start | bytes 3932168 | tf_op jit(solution)/shard_map/ppermute | solution.py:26
  183.3 79.6 %collective-permute-start.9 = (bf16[1024,640]{1,0:T(8,128)(2,1)}, bf16[1024,640]{1,0:T(8,128)(2,1)S(1)}, u32[]{:S(2)}, u32[]{:S(2)}) collective-permute-start(bf16[1024,640]{1,0:T(8,128)(2,1)} %collective-permute-done.8), channel_id=1, source_target_pairs={{0,32},{32,0},{8,40},{40,8},{16,48},{48,16},{24,56},{56,24},{64,96... | collective-permute-start | bytes 3932168 | tf_op jit(solution)/shard_map/ppermute | solution.py:26
  211.4 78.8 %collective-permute-start.4 = (bf16[1024,640]{1,0:T(8,128)(2,1)}, bf16[1024,640]{1,0:T(8,128)(2,1)S(1)}, u32[]{:S(2)}, u32[]{:S(2)}) collective-permute-start(bf16[1024,640]{1,0:T(8,128)(2,1)} %collective-permute-done.3), channel_id=1, source_target_pairs={{0,32},{32,0},{8,40},{40,8},{16,48},{48,16},{24,56},{56,24},{64,96... | collective-permute-start | bytes 3932168 | tf_op jit(solution)/shard_map/ppermute | solution.py:26
  262.8 88.6 %collective-permute-start.10 = (bf16[1024,640]{1,0:T(8,128)(2,1)S(1)}, bf16[1024,640]{1,0:T(8,128)(2,1)}, u32[]{:S(2)}, u32[]{:S(2)}) collective-permute-start(bf16[1024,640]{1,0:T(8,128)(2,1)S(1)} %collective-permute-done.9), channel_id=1, source_target_pairs={{0,64},{64,0},{8,72},{72,8},{16,80},{80,16},{24,88},{88,24},{32,96... | collective-permute-start | bytes 3932168 | tf_op jit(solution)/shard_map/ppermute | solution.py:26
  290.1 115.8 %collective-permute-start.5 = (bf16[1024,640]{1,0:T(8,128)(2,1)S(1)}, bf16[1024,640]{1,0:T(8,128)(2,1)}, u32[]{:S(2)}, u32[]{:S(2)}) collective-permute-start(bf16[1024,640]{1,0:T(8,128)(2,1)S(1)} %collective-permute-done.4), channel_id=1, source_target_pairs={{0,64},{64,0},{8,72},{72,8},{16,80},{80,16},{24,88},{88,24},{32,96... | collective-permute-start | bytes 3932168 | tf_op jit(solution)/shard_map/ppermute | solution.py:26
  351.4 150.9 %collective-permute-start.11 = (bf16[1024,640]{1,0:T(8,128)(2,1)}, bf16[1024,640]{1,0:T(8,128)(2,1)S(1)}, u32[]{:S(2)}, u32[]{:S(2)}) collective-permute-start(bf16[1024,640]{1,0:T(8,128)(2,1)} %collective-permute-done.10), channel_id=1, source_target_pairs={{0,128},{128,0},{8,136},{136,8},{16,144},{144,16},{24,152},{152,24... | collective-permute-start | bytes 3932168 | tf_op jit(solution)/shard_map/ppermute | solution.py:26
  405.9 147.6 %collective-permute-start.6 = (bf16[1024,640]{1,0:T(8,128)(2,1)}, bf16[1024,640]{1,0:T(8,128)(2,1)S(1)}, u32[]{:S(2)}, u32[]{:S(2)}) collective-permute-start(bf16[1024,640]{1,0:T(8,128)(2,1)} %collective-permute-done.5), channel_id=1, source_target_pairs={{0,128},{128,0},{8,136},{136,8},{16,144},{144,16},{24,152},{152,24... | collective-permute-start | bytes 3932168 | tf_op jit(solution)/shard_map/ppermute | solution.py:26
Sparse Core Ops, SparseCore 0:
  9.8 63.2 all-gather.1
  106.4 79.6 reduce-scatter.7
  188.7 39.8 reduce-scatter.5
  231.2 50.1 reduce-scatter.3
where the time goes:
time: 562 us; the launch traced here: 561 us
  waiting for transfers between devices  216 us (38%)
  starting transfers between devices  195 us (35%)
  blocking collectives  70.7 us (13%)
  matrix products  30.7 us (5%)
  other arithmetic  23.5 us (4%)
  between operations  16 us (3%)
  local copies, waits for them, and re-layouts  9.3 us (2%)
    ppermute x10, waiting for transfers between devices, swapped(): return lax.ppermute(block, axis, route)  216 us
    ppermute x10, starting transfers between devices, swapped(): return lax.ppermute(block, axis, route)  193 us
    all_gather x1, blocking collectives, body(): lax.all_gather(film_weight, 'fsdp', axis=1, tiled=True)  38.2 us
    all_gather x1, blocking collectives, body(): lax.all_gather(point_weight, 'fsdp', axis=1, tiled=True)  32.5 us
    dot_general x3, matrix products, unet_block(): jnp.dot(stacked, temporal_weight, preferred_element_type=jnp.float32)  16 us
    dot_general x3, matrix products, unet_block(): jnp.dot(gated, point_weight, preferred_element_type=jnp.float32)  14.3 us
  transfers between devices with their start and end apart: 16, of which 8 were waited for; matrix products, arithmetic and copies ran while one was open for 11% of the time, Pallas kernels for 0%

commit v1 on v0

--- a/solution.py
+++ b/solution.py
@@ -14,16 +14,6 @@
 def passed_along(x, axis, by):
     length = lax.axis_size(axis)
     return lax.ppermute(x, axis, [(i, (i + by) % length) for i in range(length)])
-
-
-def swapped(block, axis, stride):
-    count = lax.axis_size(axis)
-    route = []
-    for low in range(count):
-        high = low | 1 << stride
-        if high != low and high < count:
-            route += [(low, high), (high, low)]
-    return lax.ppermute(block, axis, route)
 
 
 def lookup_level(level_embed, level_index):
@@ -72,7 +62,6 @@
 ):
     sections = lax.axis_size("section")
     midpoint = sections // 2
-    bit_total = sections.bit_length() - 1
     encoder_side = lax.axis_index("section") < midpoint
     full_temporal, full_point, full_film = (
         lax.all_gather(temporal_weight, "fsdp", axis=1, tiled=True),
@@ -87,7 +76,6 @@
     hidden_forward = time_hidden(timesteps_forward[0], level_row)
     hidden_backward = time_hidden(timesteps_backward[0], level_row)
     stash_rows = stashed_input[0].astype(jnp.float32)
-    zero_rows = jnp.zeros(handoff.shape[1:], jnp.bfloat16)
 
     def backward(output_grad):
 
@@ -110,14 +98,9 @@
     section_out = unet_block(
         forward_input, hidden_forward, full_temporal, full_point, full_film
     ).astype(jnp.bfloat16)
-    sent_rows = jnp.where(encoder_side, section_out, zero_rows)
-    for bit_number in range(bit_total):
-        sent_rows = swapped(sent_rows, "section", bit_number)
     input_grad, weight_grads = backward(backward_grad)
-    sent_grad = jnp.where(encoder_side, zero_rows, input_grad)
-    for bit_number in range(bit_total):
-        sent_grad = swapped(sent_grad, "section", bit_number)
-    skip_next = jnp.where(encoder_side, sent_grad, sent_rows)
+    leaving = jnp.where(encoder_side, section_out, input_grad)
+    skip_next = lax.ppermute(leaving, "section", [(i, sections - 1 - i) for i in range(sections)])
     temporal_grad, pointwise_grad, film_grad = (
         lax.psum_scatter(
             weight_grads[0][None].astype(jnp.bfloat16), "fsdp", scatter_dimension=1, tiled=True

time: 562 us -> 321 us (0.57)
  starting transfers between devices: 195 us -> 41 us
  waiting for transfers between devices: 216 us -> 136 us
  blocking collectives: 70.7 us -> 62.6 us
    ppermute x10 -> x1, waiting for transfers between devices: 216 us -> 45.8 us  [body(): lax.ppermute(leaving, 'section', [(i, sections - 1 - i) for i in range(se...]
    ppermute x10 -> x1, starting transfers between devices: 193 us -> 40.3 us  [body(): lax.ppermute(leaving, 'section', [(i, sections - 1 - i) for i in range(se...]
    reduce_scatter x1, waiting for transfers between devices: 0.01 us -> 52.3 us  [body(): lax.psum_scatter(weight_grads[0][None].astype(jnp.bfloat16), 'fsdp', scat...]
    reduce_scatter x1, waiting for transfers between devices: 0.01 us -> 28.2 us  [body(): lax.psum_scatter(weight_grads[1][None].astype(jnp.bfloat16), 'fsdp', scat...]
    ppermute x2, waiting for transfers between devices: 0.01 us -> 9.12 us  [passed_along(): lax.ppermute(x, axis, [(i, (i + by) % length) for i in range(length)])]
    all_gather x1, blocking collectives: 38.2 us -> 30.7 us  [body(): lax.all_gather(film_weight, 'fsdp', axis=1, tiled=True)]
  transfers between devices with their start and end apart: 16 -> 7, of which waited for: 8 -> 4; matrix products, arithmetic and copies ran while one was open for 11% -> 16% of each run, Pallas kernels for 0% -> 0%
where the time goes in v1:
time: 321 us; the launch traced here: 318 us
  waiting for transfers between devices  136 us (42%)
  blocking collectives  62.6 us (20%)
  starting transfers between devices  41 us (13%)
  matrix products  35.5 us (11%)
  other arithmetic  18.1 us (6%)
  between operations  16 us (5%)
  local copies, waits for them, and re-layouts  8.61 us (3%)
    reduce_scatter x1, waiting for transfers between devices, body(): lax.psum_scatter(weight_grads[0][None].astype(jnp.bfloat16), 'fsdp', scat...  52.3 us
    ppermute x1, waiting for transfers between devices, body(): lax.ppermute(leaving, 'section', [(i, sections - 1 - i) for i in range(se...  45.8 us
    ppermute x1, starting transfers between devices, body(): lax.ppermute(leaving, 'section', [(i, sections - 1 - i) for i in range(se...  40.3 us
    all_gather x1, blocking collectives, body(): lax.all_gather(point_weight, 'fsdp', axis=1, tiled=True)  31.8 us
    all_gather x1, blocking collectives, body(): lax.all_gather(film_weight, 'fsdp', axis=1, tiled=True)  30.7 us
    reduce_scatter x1, waiting for transfers between devices, body(): lax.psum_scatter(weight_grads[1][None].astype(jnp.bfloat16), 'fsdp', scat...  28.2 us
    dot_general x3, matrix products, unet_block(): jnp.dot(gated, point_weight, preferred_element_type=jnp.float32)  18.2 us
    dot_general x3, matrix products, unet_block(): jnp.dot(stacked, temporal_weight, preferred_element_type=jnp.float32)  16.8 us
  transfers between devices with their start and end apart: 7, of which 4 were waited for; matrix products, arithmetic and copies ran while one was open for 16% of the time, Pallas kernels for 0%

profile of v1, /device:TPU:30, one launch (start us, length us, event | category | flops | bytes accessed | tf_op | source)
XLA Modules:
  0.0 317.9 jit_solution(12945800293730786802)
XLA Ops:
  7.2 0.0 all-gather.2.cloned.1.call-start
  7.2 0.7 all-gather.2.cloned.1.call-update
  7.9 0.0 reduce-scatter.8.cloned.1.call-start
  8.0 0.3 collective-permute-start.1
  10.2 0.1 fusion.75
  10.2 0.1 fusion.73
  10.3 0.8 multiply_reduce_fusion.2
  11.1 1.6 multiply_reduce_fusion
  12.7 0.1 add.200
  12.8 30.7 %all_gather.9 = bf16[1,256,1280]{2,1,0:T(8,128)(2,1)S(1)} all-gather(bf16[1,32,1280]{2,1,0:T(8,128)(2,1)} %param.21), channel_id=1, replica_groups=mesh['section'=32,'fsdp'=8] {'fsdp'}, dimensions={1}, use_global_device_ids=true | all-gather | bytes 737280 | tf_op jit(solution)/shard_map/all_gather | solution.py:69
  43.6 0.2 fusion.63
  43.8 0.5 add_convert_fusion
  44.3 0.3 fusion.91
  44.6 1.2 concatenate.48
  45.8 1.2 concatenate.50
  47.0 1.5 fusion.19
  48.5 31.8 %all_gather.11 = bf16[1,640,640]{2,1,0:T(8,128)(2,1)} all-gather(bf16[1,80,640]{2,1,0:T(8,128)(2,1)S(1)} %copy-done.8), channel_id=1, replica_groups=mesh['section'=32,'fsdp'=8] {'fsdp'}, dimensions={1}, use_global_device_ids=true | all-gather | bytes 921600 | tf_op jit(solution)/shard_map/all_gather | solution.py:68
  80.4 6.0 %fusion.29 = f32[1024,640]{1,0:T(8,128)S(1)} fusion(bf16[1,1920,640]{2,1,0:T(8,128)(2,1)} %all-gather.2.cloned.1.call-done, bf16[1024,640]{1,0:T(8,128)(2,1)} %bitcast.103, bf16[1024,640]{1,0:T(8,128)(2,1)} %fusion.19, bf16[1024,640]{1,0:T(8,128)(2,1)} %bitcast.101), kind=kOutput, calls=%fused_computation.53 | convolution fusion | flops 2528378880 | bytes 9011200 | tf_op jit(solution)/shard_map/jvp()/dot_general | solution.py:45
  86.4 1.5 copy-done.10
  87.9 1.6 fusion.12
  89.5 3.6 %convolution_convert_fusion = bf16[1024,1920]{1,0:T(8,128)(2,1)S(1)} fusion(bf16[1024,640]{1,0:T(8,128)(2,1)S(1)} %fusion.12, bf16[1,1920,640]{2,1,0:T(8,128)(2,1)S(1)} %copy-done.9), kind=kOutput, calls=%fused_computation.12 | convolution fusion | flops 2516582400 | bytes 7700480 | tf_op jit(solution)/shard_map/transpose(jvp())/dot_general | solution.py:45
  93.1 0.4 fusion.90
  93.5 1.7 fusion.14
  95.2 1.0 fusion.62
  96.2 0.0 reduce-scatter.6.cloned.1.call-start
  96.3 4.9 %fusion.47 = bf16[1,640,640]{2,1,0:T(8,128)(2,1)} fusion(bf16[1,1024,640]{2,1,0:T(8,128)(2,1)} %param.14, bf16[1,1024,640]{2,1,0:T(8,128)(2,1)} %copy-done.4, pred[]{:T(512)S(6)} %lt.3, f32[1024,640]{1,0:T(8,128)} %copy-done.10), kind=kOutput, calls=%fused_computation.67 | convolution fusion | flops 845168640 | bytes 6062081 | tf_op jit(solution)/shard_map/transpose(jvp())/dot_general | solution.py:47
  101.2 0.0 reduce-scatter.4.cloned.1.call-start
  101.3 0.3 collective-permute-start
  101.5 0.2 fusion.65
  101.8 7.2 %fusion.8 = bf16[1,1920,640]{2,1,0:T(8,128)(2,1)} fusion(bf16[1024,640]{1,0:T(8,128)(2,1)} %copy-done.11, bf16[1024,640]{1,0:T(8,128)(2,1)} %bitcast.104, bf16[1024,640]{1,0:T(8,128)(2,1)} %fusion.19, bf16[1024,640]{1,0:T(8,128)(2,1)} %bitcast.102), kind=kOutput, calls=%fused_computation.20 | convolution fusion | flops 2528378880 | bytes 7700480 | tf_op jit(solution)/shard_map/transpose(jvp())/dot_general | solution.py:45
  109.1 0.6 add_add_fusion
  109.7 9.1 %collective-permute-done = bf16[1,1024,640]{2,1,0:T(8,128)(2,1)} collective-permute-done((bf16[1,1024,640]{2,1,0:T(8,128)(2,1)}, bf16[1,1024,640]{2,1,0:T(8,128)(2,1)}, u32[]{:S(2)}, u32[]{:S(2)}) %collective-permute-start) | collective-permute-done | bytes 1310752 | tf_op jit(solution)/shard_map/ppermute | solution.py:16
  118.9 3.3 %multiply_reduce_fusion.1 = (f32[1024]{0:T(1024)S(1)}, f32[1,1024,640]{2,1,0:T(8,128)S(1)}, bf16[1,1024,640]{2,1,0:T(8,128)(2,1)}) fusion(bf16[1,1024,640]{2,1,0:T(8,128)(2,1)S(1)} %copy-done.3, pred[]{:T(512)S(6)} %lt.3, bf16[1,1024,640]{2,1,0:T(8,128)(2,1)} %collective-permute-done, f32[1,16,64,640]{3,2,1,0:T(8,128)S(1)} %add_add_fusion, ...), kind=kLoop, calls=%fused_computation.51 | loop fusion | flops 7207936 | bytes 10489857 | tf_op jit(solution)/shard_map/reduce_sum | solution.py:38
  122.2 0.1 rsqrt.27
  122.3 0.4 add_convert_fusion.1
  122.7 0.3 fusion.92
  123.0 1.2 concatenate.42
  124.2 1.2 concatenate.44
  125.4 1.5 fusion.26
  126.9 11.7 %fusion.40 = (bf16[1024,640]{1,0:T(8,128)(2,1)}, bf16[1024,640]{1,0:T(8,128)(2,1)}) fusion(f32[1,16,64,640]{3,2,1,0:T(8,128)} %copy-done.1, bf16[1,1024,640]{2,1,0:T(8,128)(2,1)} %param.14, bf16[1,1024,640]{2,1,0:T(8,128)(2,1)} %copy-done.4, pred[]{:T(512)S(6)} %lt.3, bf16[1,640,640]{2,1,0:T(8,128)(2,1)S(1)} %copy-done.7, ...), kind=kOutput, calls=%fused_computation.58 | convolution fusion | flops 3376414720 | bytes 17694720 | tf_op jit(solution)/shard_map/dot_general | solution.py:47
  138.7 40.3 %collective-permute-start.2 = (bf16[1024,640]{1,0:T(8,128)(2,1)}, bf16[1024,640]{1,0:T(8,128)(2,1)S(1)}, u32[]{:S(2)}, u32[]{:S(2)}) collective-permute-start(bf16[1024,640]{1,0:T(8,128)(2,1)} %get-tuple-element.28), channel_id=1, source_target_pairs={{0,248},{8,240},{16,232},{24,224},{32,216},{40,208},{48,200},{56,1... | collective-permute-start | bytes 3932168 | tf_op jit(solution)/shard_map/ppermute | solution.py:103
  179.0 45.8 %collective-permute-done.2 = bf16[1024,640]{1,0:T(8,128)(2,1)S(1)} collective-permute-done((bf16[1024,640]{1,0:T(8,128)(2,1)}, bf16[1024,640]{1,0:T(8,128)(2,1)S(1)}, u32[]{:S(2)}, u32[]{:S(2)}) %collective-permute-start.2) | collective-permute-done | bytes 1310752 | tf_op jit(solution)/shard_map/ppermute | solution.py:103
  224.8 1.6 convert_element_type.230
  226.3 28.2 %reduce-scatter.6.cloned.1.call-done = bf16[1,80,640]{2,1,0:T(8,128)(2,1)} async-done(((bf16[1,640,640]{2,1,0:T(8,128)(2,1)}), bf16[1,80,640]{2,1,0:T(8,128)(2,1)}) %reduce-scatter.6.cloned.1.call-update) | async-done | bytes 102416 | tf_op jit(solution)/shard_map/reduce_scatter | solution.py:108
  254.5 1.6 convert_element_type.227
  256.1 52.3 %reduce-scatter.4.cloned.1.call-done = bf16[1,240,640]{2,1,0:T(8,128)(2,1)} async-done(((bf16[1,1920,640]{2,1,0:T(8,128)(2,1)}), bf16[1,240,640]{2,1,0:T(8,128)(2,1)}) %reduce-scatter.4.cloned.1.call-update) | async-done | bytes 307216 | tf_op jit(solution)/shard_map/reduce_scatter | solution.py:105
  308.4 1.8 convert_element_type.223
  310.3 1.1 copy.21
  (42 shorter events, 0.3 us)
Async XLA Ops:
  7.2 36.6 %copy-start = (bf16[1,1024,640]{2,1,0:T(8,128)(2,1)S(1)}, bf16[1,1024,640]{2,1,0:T(8,128)(2,1)}, u32[]{:S(2)}) copy-start(bf16[1,1024,640]{2,1,0:T(8,128)(2,1)} %param.13) | copy-start | bytes 3932164
  7.2 73.2 %all-gather.2.cloned.1.call-start = ((), (), s32[]{:S(2)}) async-start(), calls=%async_computation.3 | async-start | bytes 2764800 | tf_op jit(solution)/shard_map/all_gather | solution.py:67
  7.9 216.8 %reduce-scatter.8.cloned.1.call-start = ((), (), s32[]{:S(2)}) async-start(), calls=%async_computation.6 | async-start | bytes 737280 | tf_op jit(solution)/shard_map/reduce_scatter | solution.py:111
  8.0 78.5 %collective-permute-start.1 = (bf16[1,1024,640]{2,1,0:T(8,128)(2,1)}, bf16[1,1024,640]{2,1,0:T(8,128)(2,1)S(1)}, u32[]{:S(2)}, u32[]{:S(2)}) collective-permute-start(bf16[1,1024,640]{2,1,0:T(8,128)(2,1)} %param.12), channel_id=1, source_target_pairs={{0,248},{8,0},{16,8},{24,16},{32,24},{40,32},{48,40},{56,48},{64,5... | collective-permute-start | bytes 3932168 | tf_op jit(solution)/shard_map/ppermute | solution.py:16
  45.8 2.7 copy-start.8
  80.4 7.5 %copy-start.2 = (bf16[1,1024,640]{2,1,0:T(8,128)(2,1)S(1)}, bf16[1,1024,640]{2,1,0:T(8,128)(2,1)}, u32[]{:S(2)}) copy-start(bf16[1,1024,640]{2,1,0:T(8,128)(2,1)} %param.14) | copy-start | bytes 3932164
  80.4 7.5 %copy-start.6 = (bf16[1,640,640]{2,1,0:T(8,128)(2,1)S(1)}, bf16[1,640,640]{2,1,0:T(8,128)(2,1)}, u32[]{:S(2)}) copy-start(bf16[1,640,640]{2,1,0:T(8,128)(2,1)} %all_gather.11) | copy-start | bytes 2457604
  86.4 1.5 copy-start.10
  86.4 3.1 copy-start.9
  87.9 1.6 copy-start.4
  89.5 3.6 %copy-start.11 = (bf16[1024,640]{1,0:T(8,128)(2,1)}, bf16[1024,640]{1,0:T(8,128)(2,1)S(1)}, u32[]{:S(2)}) copy-start(bf16[1024,640]{1,0:T(8,128)(2,1)S(1)} %fusion.12) | copy-start | bytes 3932164
  96.2 158.3 %reduce-scatter.6.cloned.1.call-start = ((), (), s32[]{:S(2)}) async-start(), calls=%async_computation.5 | async-start | bytes 921600 | tf_op jit(solution)/shard_map/reduce_scatter | solution.py:108
  101.2 207.2 %reduce-scatter.4.cloned.1.call-start = ((), (), s32[]{:S(2)}) async-start(), calls=%async_computation.4 | async-start | bytes 2764800 | tf_op jit(solution)/shard_map/reduce_scatter | solution.py:105
  101.3 17.6 %collective-permute-start = (bf16[1,1024,640]{2,1,0:T(8,128)(2,1)}, bf16[1,1024,640]{2,1,0:T(8,128)(2,1)}, u32[]{:S(2)}, u32[]{:S(2)}) collective-permute-start(bf16[1,1024,640]{2,1,0:T(8,128)(2,1)} %param.11), channel_id=1, source_target_pairs={{0,8},{8,16},{16,24},{24,32},{32,40},{40,48},{48,56},{56,64},{64,7... | collective-permute-start | bytes 3932168 | tf_op jit(solution)/shard_map/ppermute | solution.py:16
  109.1 9.8 %copy-start.3 = (bf16[1,1024,640]{2,1,0:T(8,128)(2,1)S(1)}, bf16[1,1024,640]{2,1,0:T(8,128)(2,1)}, u32[]{:S(2)}) copy-start(bf16[1,1024,640]{2,1,0:T(8,128)(2,1)} %param.14) | copy-start | bytes 3932164
  109.1 9.8 %copy-start.5 = (bf16[1,1024,640]{2,1,0:T(8,128)(2,1)S(1)}, bf16[1,1024,640]{2,1,0:T(8,128)(2,1)}, u32[]{:S(2)}) copy-start(bf16[1,1024,640]{2,1,0:T(8,128)(2,1)} %copy-done.4) | copy-start | bytes 3932164
  109.7 9.1 %copy-start.1 = (f32[1,16,64,640]{3,2,1,0:T(8,128)}, f32[1,16,64,640]{3,2,1,0:T(8,128)S(1)}, u32[]{:S(2)}) copy-start(f32[1,16,64,640]{3,2,1,0:T(8,128)S(1)} %add_add_fusion) | copy-start | bytes 7864324
  124.2 2.7 copy-start.7
  138.7 86.1 %collective-permute-start.2 = (bf16[1024,640]{1,0:T(8,128)(2,1)}, bf16[1024,640]{1,0:T(8,128)(2,1)S(1)}, u32[]{:S(2)}, u32[]{:S(2)}) collective-permute-start(bf16[1024,640]{1,0:T(8,128)(2,1)} %get-tuple-element.28), channel_id=1, source_target_pairs={{0,248},{8,240},{16,232},{24,224},{32,216},{40,208},{48,200},{56,1... | collective-permute-start | bytes 3932168 | tf_op jit(solution)/shard_map/ppermute | solution.py:103
Sparse Core Ops, SparseCore 0:
  9.8 47.6 all-gather.1
  96.3 98.5 reduce-scatter.7
  197.5 56.9 reduce-scatter.5
  257.1 51.2 reduce-scatter.3

commit v2 on v1

v2 whole, which is shorter than its diff:
```python
import functools
import math

import jax
import jax.numpy as jnp
from jax import lax
from jax.experimental import pallas as pl
from jax.experimental.pallas import tpu as pltpu
from jax.sharding import PartitionSpec as P

FRAMES = 16
LEVELS = 4
RING = 4
EPS = 1e-06
F32 = jnp.float32
BF16 = jnp.bfloat16
MESH = pl.DeviceIdType.MESH


def lookup_level(level_embed, level_index):
    onehot = (jnp.arange(LEVELS, dtype=jnp.int32) == level_index).astype(F32)
    return jnp.sum(onehot[:, None] * level_embed, axis=0)


def time_hidden(timesteps, level_row):
    half_width = level_row.shape[0] // 2
    frequency = jnp.exp(-math.log(10000.0) * jnp.arange(half_width, dtype=F32) / half_width)
    phases = timesteps.astype(F32)[:, None] * frequency[None, :]
    embedded = jnp.concatenate([jnp.sin(phases), jnp.cos(phases)], axis=-1) + level_row[None, :]
    return jax.nn.silu(embedded).astype(BF16)


def sigmoid(t):
    return 0.5 + 0.5 * jnp.tanh(0.5 * t)


def nt(a, b):
    return lax.dot_general(a, b, (((1,), (1,)), ((), ())), preferred_element_type=F32)


def dot(a, b):
    return jnp.dot(a, b, preferred_element_type=F32)


def tick(
    sections,
    hid, handoff, returning, stash, held, tw_in, pw_in, fw_in,
    out_f, out_b, out_skip, out_tg, out_pg, out_fg,
    arrived, back, stash_v, held_v, tw, pw, fwpad, hid_all, part, film_in, film,
    modf, modb, dtp, gated, gb, fout, bout, mod_t, gated_t, grad,
    ra_p, ra_m, rb_p, rb_m, zsend, zrecv, sums, dfilm, fg, tg, pg,
    load_sem, move_send, move_recv, hid_send, hid_recv, part_send, part_recv,
    df_send, df_recv, ag_send, ag_recv, skip_send, skip_recv, rs_send, rs_recv, out_sem, go,
):
    rows, ch = arrived.shape
    cell = rows // FRAMES
    chunk = rows // 4
    small = cell
    tws, pws, fws = tw_in.shape[1], pw_in.shape[1], fw_in.shape[1]
    n_fsdp = 2 * RING
    s, f = lax.axis_index("section"), lax.axis_index("fsdp")
    z, x = f // RING, f % RING
    xp, xm, x2 = (x + 1) % RING, (x + RING - 1) % RING, (x + 2) % RING
    zo = 1 - z
    fz, fxp, fxm = zo * RING + x, z * RING + xp, z * RING + xm
    ahead, behind, mirror = (s + 1) % sections, (s + sections - 1) % sections, sections - 1 - s
    core = s % 2
    sibling = s + 1 - 2 * core
    is_enc = s < sections // 2
    enc = jnp.where(is_enc, 1, 0)
    first = core == enc
    enc_f = enc.astype(F32)

    def at(section, fsdp):
        return {"section": section, "fsdp": fsdp}

    def remote(src, dst, send, recv, section, fsdp):
        return pltpu.make_async_remote_copy(
            src_ref=src, dst_ref=dst, send_sem=send, recv_sem=recv,
            device_id=at(section, fsdp), device_id_type=MESH,
        )

    fwpad[...] = jnp.zeros_like(fwpad)
    loads = [
        pltpu.make_async_copy(fw_in.at[0], fwpad.at[pl.ds(f * fws, fws)], load_sem.at[0]),
        pltpu.make_async_copy(stash.at[0], stash_v, load_sem.at[1]),
        pltpu.make_async_copy(held.at[0], held_v, load_sem.at[2]),
        pltpu.make_async_copy(tw_in.at[0], tw.at[pl.ds(f * tws, tws)], load_sem.at[3]),
        pltpu.make_async_copy(pw_in.at[0], pw.at[pl.ds(f * pws, pws)], load_sem.at[4]),
        pltpu.make_async_copy(hid, hid_all.at[:, f], load_sem.at[5]),
    ]
    for load in loads:
        load.start()

    barrier = pltpu.get_barrier_semaphore()
    for section in (ahead, behind, mirror):
        pl.semaphore_signal(barrier, inc=1, device_id=at(section, f), device_id_type=MESH)
    for d in range(1, n_fsdp):
        pl.semaphore_signal(barrier, inc=1, device_id=at(s, (f + d) % n_fsdp), device_id_type=MESH)
    pl.semaphore_wait(barrier, 3 + n_fsdp - 1)

    hid_out = [
        remote(hid, hid_all.at[:, f], hid_send.at[d], hid_recv.at[d], s, (f + d) % n_fsdp)
        for d in range(1, n_fsdp)
    ]
    for copy in hid_out:
        copy.start()

    h0 = {tws: (tws // 2 + 15) // 16 * 16, pws: pws // 2 // 16 * 16}

    def ag_copies(i, src_own, full, n):
        lo, hi = h0[n], n - h0[n]

        def shard(index):
            return full.at[pl.ds(index * n, n)]

        def low(index):
            return full.at[pl.ds(index * n, lo)]

        def high(index):
            return full.at[pl.ds(index * n + lo, hi)]

        fo_p, fo_m = zo * RING + xp, zo * RING + xm
        f_2, fo_2 = z * RING + x2, zo * RING + x2
        plan = [
            (src_own.at[0], shard(f), shard(fz), fz),
            (src_own.at[0], shard(f), shard(fxm), fxp),
            (src_own.at[0], shard(f), shard(fxp), fxm),
            (shard(fz), shard(fz), shard(fo_m), fxp),
            (shard(fz), shard(fz), shard(fo_p), fxm),
            (low(fxm), low(fxm), low(f_2), fxp),
            (high(fxp), high(fxp), high(f_2), fxm),
            (low(fo_m), low(fo_m), low(fo_2), fxp),
            (high(fo_p), high(fo_p), high(fo_2), fxm),
        ]
        sends, recvs = [], []
        for k, (src, dst, land, target) in enumerate(plan):
            sends.append(remote(src, dst, ag_send.at[i, k], ag_recv.at[i, k], s, target))
            recvs.append(remote(land, land, ag_send.at[i, k], ag_recv.at[i, k], s, target))
        return sends, recvs

    tw_sends, tw_recvs = ag_copies(0, tw_in, tw, tws)
    pw_sends, pw_recvs = ag_copies(1, pw_in, pw, pws)

    def ag_begin():
        for k in range(3):
            tw_sends[k].start()
        for k in range(3):
            pw_sends[k].start()

    pl.when(first)(ag_begin)

    move_f = remote(handoff.at[0], arrived, move_send.at[0], move_recv.at[0], ahead, f)
    move_b = remote(returning.at[0], back, move_send.at[1], move_recv.at[1], behind, f)
    move_f.start()
    move_b.start()

    for padded in (modf, modb, dtp):
        padded[0:cell] = jnp.zeros((cell, ch), BF16)
        padded[cell + rows : 2 * cell + rows] = jnp.zeros((cell, ch), BF16)

    loads[0].wait()
    loads[5].wait()
    for d in range(1, n_fsdp):
        came = (f + n_fsdp - d) % n_fsdp
        remote(hid, hid_all.at[:, came], hid_send.at[d], hid_recv.at[d], s, came).wait_recv()
    hidden = jnp.concatenate(
        [hid_all[r, j] for r in range(2) for j in range(n_fsdp)], axis=0
    ).astype(BF16)
    partial = dot(hidden, fwpad[...])
    for r in range(2):
        for j in range(n_fsdp):
            k = r * n_fsdp + j
            part[j, r] = partial[k : k + 1]
    part_out = []
    for d in range(1, n_fsdp):
        j = (f + d) % n_fsdp
        part_out.append(remote(part.at[j], film_in.at[f], part_send.at[d], part_recv.at[d], s, j))
    for copy in part_out:
        copy.start()
    for d in range(1, n_fsdp):
        came = (f + n_fsdp - d) % n_fsdp
        remote(part.at[came], film_in.at[came], part_send.at[d], part_recv.at[d], s, came).wait_recv()
    film_in[f] = part[f]
    film[...] = jnp.sum(film_in[...], axis=0)

    def scale_shift(r):
        return 1.0 + film[r, :, 0:ch], film[r, :, ch : 2 * ch]

    def modulate(read, r, dst):
        scale, shift = scale_shift(r)

        def step(i, carry):
            at_row = pl.multiple_of(i * small, small)
            v = read(at_row, small)
            rstd = lax.rsqrt(jnp.mean(v * v, axis=-1, keepdims=True) + EPS)
            dst[pl.ds(at_row + cell, small)] = (v * rstd * scale + shift).astype(BF16)
            return carry

        lax.fori_loop(0, rows // small, step, 0)

    def read_stash(r0, n):
        return stash_v[pl.ds(r0, n)].astype(F32)

    def read_forward(r0, n):
        return arrived[pl.ds(r0, n)].astype(F32) + held_v[pl.ds(r0, n)].astype(F32) * (1.0 - enc_f)

    def read_grad(r0, n):
        return back[pl.ds(r0, n)].astype(F32) + held_v[pl.ds(r0, n)].astype(F32) * enc_f

    loads[1].wait()
    loads[2].wait()
    modulate(read_stash, 1, modb)

    @pl.when(jnp.logical_not(first))
    def _():
        pl.semaphore_wait(go, 1)
        ag_begin()

    for recvs, sends in ((tw_recvs, tw_sends), (pw_recvs, pw_sends)):
        recvs[0].wait_recv()
        sends[3].start()
        sends[4].start()
    for recvs, sends in ((tw_recvs, tw_sends), (pw_recvs, pw_sends)):
        recvs[1].wait_recv()
        sends[5].start()
        recvs[2].wait_recv()
        sends[6].start()
    for recvs, sends in ((tw_recvs, tw_sends), (pw_recvs, pw_sends)):
        recvs[3].wait_recv()
        sends[7].start()
        recvs[4].wait_recv()
        sends[8].start()

    @pl.when(first)
    def _():
        pl.semaphore_signal(go, inc=1, device_id=at(sibling, f), device_id_type=MESH)

    loads[3].wait()
    loads[4].wait()

    def gather_end():
        for recvs in (tw_recvs, pw_recvs):
            for k in range(5, 9):
                recvs[k].wait_recv()

    def skip_copy(src, c):
        piece = pl.ds(pl.multiple_of(c * chunk, chunk), chunk)
        return remote(src.at[piece], out_skip.at[0, piece], skip_send.at[c], skip_recv.at[c], mirror, f)

    def temporal_of(mod, r0):
        taps = [mod[pl.ds(pl.multiple_of(r0 + k * cell, cell), chunk)] for k in range(3)]
        return dot(jnp.concatenate(taps, axis=1), tw[...])

    out_f_copy = pltpu.make_async_copy(fout, out_f.at[0], out_sem.at[0])
    out_b_copy = pltpu.make_async_copy(bout, out_b.at[0], out_sem.at[1])

    def forward():
        move_f.wait_recv()
        modulate(read_forward, 0, modf)
        pl.when(is_enc)(gather_end)

        def step(c, carry):
            r0 = pl.multiple_of(c * chunk, chunk)
            t = temporal_of(modf, r0)
            gate = (t * sigmoid(t)).astype(BF16)
            fout[pl.ds(r0, chunk)] = (read_forward(r0, chunk) + dot(gate, pw[...])).astype(BF16)

            @pl.when(is_enc)
            def _():
                skip_copy(fout, c).start()

            return carry

        lax.fori_loop(0, rows // chunk, step, 0)
        out_f_copy.start()

    half = (tws + pws) // 2
    lo, hi = pl.ds(0, half), pl.ds(half, half)
    rs_plan = [
        (grad.at[:, x2, lo], ra_p, fxp, fxm),
        (grad.at[:, x2, hi], ra_m, fxm, fxp),
        (grad.at[:, xp, hi], rb_p.at[:, hi], fxp, fxm),
        (grad.at[:, xm, lo], rb_m.at[:, lo], fxm, fxp),
        (ra_p, rb_p.at[:, lo], fxp, fxm),
        (ra_m, rb_m.at[:, hi], fxm, fxp),
        (zsend, zrecv, fz, fz),
    ]
    rs = [
        remote(src, dst, rs_send.at[k], rs_recv.at[k], s, target)
        for k, (src, dst, target, _) in enumerate(rs_plan)
    ]
    df_out = [
        remote(dfilm.at[f], dfilm.at[f], df_send.at[d], df_recv.at[d], s, (f + d) % n_fsdp)
        for d in range(1, n_fsdp)
    ]

    def backward():
        move_b.wait_recv()
        pl.when(jnp.logical_not(is_enc))(gather_end)
        sums[...] = jnp.zeros_like(sums)
        scale, _ = scale_shift(1)

        def step(c, carry):
            @pl.when(c < rows // chunk)
            def _():
                r0 = pl.multiple_of(c * chunk, chunk)
                t = temporal_of(modb, r0)
                sig = sigmoid(t)
                gated[pl.ds(r0, chunk)] = (t * sig).astype(BF16)
                g = read_grad(r0, chunk).astype(BF16)
                gb[pl.ds(r0, chunk)] = g
                dgate = nt(g, pw[...]).astype(BF16).astype(F32)
                dtp[pl.ds(pl.multiple_of(r0 + cell, cell), chunk)] = (
                    dgate * (sig * (1.0 + t * (1.0 - sig)))
                ).astype(BF16)

            @pl.when(c >= 1)
            def _():
                r0 = pl.multiple_of((c - 1) * chunk, chunk)
                dmod = jnp.zeros((chunk, ch), F32)
                for k in range(3):
                    piece = dtp[pl.ds(pl.multiple_of(r0 + (2 - k) * cell, cell), chunk)]
                    dmod += nt(piece, tw[k * ch : (k + 1) * ch])
                v = read_stash(r0, chunk)
                rstd = lax.rsqrt(jnp.mean(v * v, axis=-1, keepdims=True) + EPS)
                normalized = v * rstd
                sums[0] += jnp.sum((dmod * normalized).reshape(chunk // 8, 8, ch), axis=0)
                sums[1] += jnp.sum(dmod.reshape(chunk // 8, 8, ch), axis=0)
                dn = dmod * scale
                along = jnp.mean(dn * normalized, axis=-1, keepdims=True)
                bout[pl.ds(r0, chunk)] = (
                    read_grad(r0, chunk) + rstd * (dn - normalized * along)
                ).astype(BF16)

                @pl.when(jnp.logical_not(is_enc))
                def _():
                    skip_copy(bout, c - 1).start()

            return carry

        lax.fori_loop(0, rows // chunk + 1, step, 0)
        out_b_copy.start()
        dfilm[f] = jnp.concatenate(
            [jnp.sum(sums[0], axis=0, keepdims=True), jnp.sum(sums[1], axis=0, keepdims=True)], axis=1
        )
        for copy in df_out:
            copy.start()

        def turn(i, carry):
            cols = pl.ds(pl.multiple_of(i * 128, 128), 128)
            mod_t[cols] = modb[pl.ds(cell, rows), cols].T
            gated_t[cols] = gated[:, cols].T
            return carry

        lax.fori_loop(0, ch // 128, turn, 0)
        block = ch // 8
        for part_no in range(2):
            mrows = slice(part_no * ch // 2, (part_no + 1) * ch // 2)
            value = dot(gated_t[mrows], gb[...]).astype(BF16)
            for i in range(4):
                b = part_no * 4 + i
                grad[b // RING, b % RING, tws : tws + pws] = value[i * block : (i + 1) * block]
            for k in range(3):
                value = dot(mod_t[mrows], dtp[(2 - k) * cell : (2 - k) * cell + rows]).astype(BF16)
                for i in range(4):
                    b = k * 8 + part_no * 4 + i
                    j = b // 3
                    grad[j // RING, j % RING, (b % 3) * block : (b % 3 + 1) * block] = value[
                        i * block : (i + 1) * block
                    ]
        for k in range(4):
            rs[k].start()

    def phase(p, carry):
        which = p + enc
        pl.when(which == 1)(forward)
        pl.when(which != 1)(backward)
        return carry

    lax.fori_loop(0, 2, phase, 0)

    def add_rows(dst, src):
        for zi in range(2):
            dst[zi] = (dst[zi].astype(F32) + src[zi].astype(F32)).astype(BF16)

    rs[0].wait_recv()
    add_rows(ra_p, grad.at[:, xp, lo])
    rs[4].start()
    rs[1].wait_recv()
    add_rows(ra_m, grad.at[:, xm, hi])
    rs[5].start()

    for d in range(1, n_fsdp):
        came = (f + n_fsdp - d) % n_fsdp
        remote(dfilm.at[came], dfilm.at[came], df_send.at[d], df_recv.at[d], s, came).wait_recv()
    hidden_b = jnp.concatenate([hid_all[1, j] for j in range(n_fsdp)], axis=0).astype(BF16)
    dfilm_all = jnp.concatenate([dfilm[j] for j in range(n_fsdp)], axis=0).astype(BF16)
    fg[...] = lax.dot_general(hidden_b, dfilm_all, (((0,), (0,)), ((), ())), preferred_element_type=F32)
    fg_copy = pltpu.make_async_copy(fg.at[pl.ds(f * fws, fws)], out_fg.at[0], out_sem.at[2])
    fg_copy.start()

    for k in range(2, 6):
        rs[k].wait_recv()

    def along_x(zi):
        return grad[zi, x].astype(F32) + rb_p[zi].astype(F32) + rb_m[zi].astype(F32)

    zsend[...] = along_x(zo).astype(BF16)
    rs[6].start()
    own = along_x(z)
    tg[...] = own[0:tws]
    pg[...] = own[tws : tws + pws]
    rs[6].wait_recv()
    tg[...] += zrecv[0:tws].astype(F32)
    pg[...] += zrecv[tws : tws + pws].astype(F32)
    tg_copy = pltpu.make_async_copy(tg, out_tg.at[0], out_sem.at[3])
    pg_copy = pltpu.make_async_copy(pg, out_pg.at[0], out_sem.at[4])
    tg_copy.start()
    pg_copy.start()

    for copy in hid_out + part_out + df_out + tw_sends + pw_sends + rs + [move_f, move_b]:
        copy.wait_send()

    def skip_end(c, carry):
        copy = skip_copy(fout, c)
        copy.wait_send()
        copy.wait_recv()
        return carry

    lax.fori_loop(0, rows // chunk, skip_end, 0)
    for copy in (out_f_copy, out_b_copy, fg_copy, tg_copy, pg_copy):
        copy.wait()


def body(
    handoff,
    returning,
    stashed_input,
    skip_held,
    timesteps_forward,
    timesteps_backward,
    section_level,
    level_embed,
    temporal_weight,
    point_weight,
    film_weight,
):
    sections, n_fsdp = lax.axis_size("section"), lax.axis_size("fsdp")
    _, rows, ch = handoff.shape
    tws, pws, fws = temporal_weight.shape[1], point_weight.shape[1], film_weight.shape[1]
    embed = level_embed.shape[1]
    cell = rows // FRAMES
    level_row = lookup_level(level_embed, section_level[0])
    steps = jnp.concatenate([timesteps_forward[0], timesteps_backward[0]])
    hid = time_hidden(steps, level_row).astype(F32)[:, None, :]

    def vmem(shape, dtype=BF16):
        return pltpu.VMEM(shape, dtype)

    act, padded = (rows, ch), (rows + 2 * cell, ch)
    shard, half = (tws + pws, ch), ((tws + pws) // 2, ch)
    dma = pltpu.SemaphoreType.DMA
    scratch = [
        vmem(act), vmem(act), vmem(act), vmem(act),
        vmem((tws * n_fsdp, ch)), vmem((pws * n_fsdp, ch)), vmem((embed, 2 * ch)),
        vmem((2, n_fsdp, 1, embed), F32),
        vmem((n_fsdp, 2, 1, 2 * ch), F32), vmem((n_fsdp, 2, 1, 2 * ch), F32), vmem((2, 1, 2 * ch), F32),
        vmem(padded), vmem(padded), vmem(padded),
        vmem(act), vmem(act), vmem(act), vmem(act),
        vmem((ch, rows)), vmem((ch, rows)),
        vmem((2, RING) + shard),
        vmem((2,) + half), vmem((2,) + half), vmem((2,) + shard), vmem((2,) + shard),
        vmem(shard), vmem(shard),
        vmem((2, 8, ch), F32), vmem((n_fsdp, 1, 2 * ch), F32),
        vmem((embed, 2 * ch), F32), vmem((tws, ch), F32), vmem((pws, ch), F32),
        dma((6,)), dma((2,)), dma((2,)), dma((n_fsdp,)), dma((n_fsdp,)), dma((n_fsdp,)), dma((n_fsdp,)),
        dma((n_fsdp,)), dma((n_fsdp,)), dma((2, 9)), dma((2, 9)), dma((4,)), dma((4,)), dma((7,)), dma((7,)),
        dma((5,)), pltpu.SemaphoreType.REGULAR,
    ]
    hbm = pl.BlockSpec(memory_space=pl.ANY)
    local = pl.BlockSpec(memory_space=pltpu.VMEM)
    like = jax.ShapeDtypeStruct
    return tuple(
        pl.pallas_call(
            functools.partial(tick, sections),
            out_shape=(
                like(handoff.shape, BF16),
                like(handoff.shape, BF16),
                like(handoff.shape, BF16),
                like(temporal_weight.shape, F32),
                like(point_weight.shape, F32),
                like(film_weight.shape, F32),
            ),
            in_specs=[local] + [hbm] * 7,
            out_specs=(hbm,) * 6,
            scratch_shapes=scratch,
            compiler_params=pltpu.CompilerParams(
                collective_id=0, has_side_effects=True, vmem_limit_bytes=56 * 1024 * 1024
            ),
            name="relay_tick",
        )(hid, handoff, returning, stashed_input, skip_held, temporal_weight, point_weight, film_weight)
    )


def solution(mesh):
    rows = P("section", "fsdp", None)
    in_specs = (rows, rows, rows, rows, P("section", "fsdp"), P("section", "fsdp"), P("section"), P(), rows, rows, rows)
    return jax.shard_map(body, mesh=mesh, in_specs=in_specs, out_specs=(rows,) * 6, check_vma=False)
```

time: 321 us -> 136 us (0.42)
  the two profiles are of different devices: /device:TPU:30 before, /device:TPU:2 now
where the time goes in v2:
time: 136 us
  Pallas kernels  124 us (91%)
  local copies, waits for them, and re-layouts  8.03 us (6%)
  between operations  2.6 us (2%)
  other arithmetic  1.58 us (1%)
    pallas_call x1, Pallas kernels, body(): pl.pallas_call(functools.partial(tick, sections), out_shape=(like(handoff...  124 us
    unnamed x16, local copies, waits for them, and re-layouts  8.03 us

profile of v2, /device:TPU:2, one launch (start us, length us, event | category | flops | bytes accessed | tf_op | source)
XLA Modules:
  0.0 135.9 jit_solution(17852764838045332683)
XLA Ops:
  2.6 0.1 add_convert_fusion
  2.6 0.8 multiply_reduce_fusion
  3.4 0.1 multiply_sine_fusion
  3.5 0.6 convert_convert_fusion.hid
  4.2 123.7 %relay_tick.1 = (bf16[1,1024,640]{2,1,0:T(8,128)(2,1)}, bf16[1,1024,640]{2,1,0:T(8,128)(2,1)}, bf16[1,1024,640]{2,1,0:T(8,128)(2,1)}, f32[1,240,640]{2,1,0:T(8,1...) custom-call(f32[2,1,256]{2,1,0:T(1,128)} %convert_convert_fusion.hid, bf16[1,1024,640]{2,1,0:T(8,128)(2,1)} %handoff.1, ...), custom_call_target="tpu_custom_call" | custom-call | tf_op jit(solution)/shard_map/relay_tick/pallas_call | solution.py:485
  127.9 0.0 copy-start.1
  127.9 2.6 %copy.29 = bf16[1,1024,640]{2,1,0:T(8,128)(2,1)} copy(bf16[1,1024,640]{2,1,0:T(8,128)(2,1)} %get-tuple-element.14) | data formatting | bytes 2621440
  130.5 0.0 copy-done.1
  130.5 0.0 copy-start
  130.5 1.1 copy.30
  131.5 0.7 copy-done
  132.3 0.0 copy-start.2
  132.3 0.0 copy-start.3
  132.3 1.1 copy.31
  133.3 0.4 copy-done.2
  133.8 0.0 copy-start.4
  133.8 0.8 copy.32
  134.6 0.0 copy-done.3
  134.6 0.7 copy.33
  135.3 0.0 copy-done.4
  135.3 0.7 copy.34
  (2 shorter events, 0.0 us)
Async XLA Ops:
  127.9 2.6 %copy-start.1 = (bf16[1,1024,640]{2,1,0:T(8,128)(2,1)S(1)}, bf16[1,1024,640]{2,1,0:T(8,128)(2,1)}, u32[]{:S(2)}) copy-start(bf16[1,1024,640]{2,1,0:T(8,128)(2,1)} %get-tuple-element.15) | copy-start | bytes 3932164
  130.5 1.8 %copy-start = (bf16[1,1024,640]{2,1,0:T(8,128)(2,1)S(1)}, bf16[1,1024,640]{2,1,0:T(8,128)(2,1)}, u32[]{:S(2)}) copy-start(bf16[1,1024,640]{2,1,0:T(8,128)(2,1)} %get-tuple-element.16) | copy-start | bytes 3932164
  132.3 1.5 %copy-start.2 = (f32[1,240,640]{2,1,0:T(8,128)S(1)}, f32[1,240,640]{2,1,0:T(8,128)}, u32[]{:S(2)}) copy-start(f32[1,240,640]{2,1,0:T(8,128)} %get-tuple-element.17) | copy-start | bytes 1843204
  132.3 2.3 %copy-start.3 = (f32[1,80,640]{2,1,0:T(8,128)S(1)}, f32[1,80,640]{2,1,0:T(8,128)}, u32[]{:S(2)}) copy-start(f32[1,80,640]{2,1,0:T(8,128)} %get-tuple-element.18) | copy-start | bytes 614404
  133.8 1.5 %copy-start.4 = (f32[1,32,1280]{2,1,0:T(8,128)S(1)}, f32[1,32,1280]{2,1,0:T(8,128)}, u32[]{:S(2)}) copy-start(f32[1,32,1280]{2,1,0:T(8,128)} %get-tuple-element.19) | copy-start | bytes 491524

commit v3 on v2

--- a/solution.py
+++ b/solution.py
@@ -48,9 +48,10 @@
     out_f, out_b, out_skip, out_tg, out_pg, out_fg,
     arrived, back, stash_v, held_v, tw, pw, fwpad, hid_all, part, film_in, film,
     modf, modb, dtp, gated, gb, fout, bout, mod_t, gated_t, grad,
-    ra_p, ra_m, rb_p, rb_m, zsend, zrecv, sums, dfilm, fg, tg, pg,
+    ra_p, ra_m, rb_p, rb_m, zsend, zrecv, sums, dfilm, fg, tg, pg, relay_h, relay_r,
     load_sem, move_send, move_recv, hid_send, hid_recv, part_send, part_recv,
-    df_send, df_recv, ag_send, ag_recv, skip_send, skip_recv, rs_send, rs_recv, out_sem, go,
+    df_send, df_recv, ag_send, ag_recv, skip_send, skip_recv, rs_send, rs_recv, out_sem,
+    relay_send, relay_recv, go,
 ):
     rows, ch = arrived.shape
     cell = rows // FRAMES
@@ -70,6 +71,20 @@
     enc = jnp.where(is_enc, 1, 0)
     first = core == enc
     enc_f = enc.astype(F32)
+    forward_first = enc * jnp.where(first, 1, 0)
+
+    period = min(8, sections)
+    place, run = s % period, s // period
+    enc_before = jnp.where((s + sections - 1) % sections < sections // 2, 1, 0)
+    enc_after = jnp.where((s + 1) % sections < sections // 2, 1, 0)
+    far_f, far_b = place == period - 1, place == 0
+    near_f, near_b = jnp.logical_not(far_f), jnp.logical_not(far_b)
+    relay_f_at, relay_b_at = run * period + enc, run * period + period - 2 + enc
+    is_relay_f, is_relay_b = s == relay_f_at, s == relay_b_at
+    relay_f_from, relay_b_from = run * period + period - 1, run * period
+    relay_f_to, relay_b_to = (run * period + period) % sections, (run * period + sections - 1) % sections
+    relay_f_into = (run * period + sections - period) % sections + enc_before
+    relay_b_into = (run * period + period) % sections + period - 2 + enc_after
 
     def at(section, fsdp):
         return {"section": section, "fsdp": fsdp}
@@ -97,7 +112,15 @@
         pl.semaphore_signal(barrier, inc=1, device_id=at(section, f), device_id_type=MESH)
     for d in range(1, n_fsdp):
         pl.semaphore_signal(barrier, inc=1, device_id=at(s, (f + d) % n_fsdp), device_id_type=MESH)
-    pl.semaphore_wait(barrier, 3 + n_fsdp - 1)
+    greet = [(is_relay_f, relay_f_from), (is_relay_b, relay_b_from), (far_b, relay_f_into), (far_f, relay_b_into)]
+    for role, section in greet:
+        pl.when(role)(
+            functools.partial(
+                pl.semaphore_signal, barrier, inc=1, device_id=at(section, f), device_id_type=MESH
+            )
+        )
+    extra = sum(jnp.where(role, 1, 0) for role in (far_f, far_b, is_relay_f, is_relay_b))
+    pl.semaphore_wait(barrier, 3 + n_fsdp - 1 + extra)
 
     hid_out = [
         remote(hid, hid_all.at[:, f], hid_send.at[d], hid_recv.at[d], s, (f + d) % n_fsdp)
@@ -142,18 +165,42 @@
     tw_sends, tw_recvs = ag_copies(0, tw_in, tw, tws)
     pw_sends, pw_recvs = ag_copies(1, pw_in, pw, pws)
 
-    def ag_begin():
-        for k in range(3):
-            tw_sends[k].start()
-        for k in range(3):
-            pw_sends[k].start()
-
-    pl.when(first)(ag_begin)
-
-    move_f = remote(handoff.at[0], arrived, move_send.at[0], move_recv.at[0], ahead, f)
-    move_b = remote(returning.at[0], back, move_send.at[1], move_recv.at[1], behind, f)
-    move_f.start()
-    move_b.start()
+    def start(pairs, ks):
+        for k in ks:
+            for sends in pairs:
+                sends[k].start()
+
+    both = (tw_sends, pw_sends)
+    later = jnp.logical_not(first)
+
+    @pl.when(first)
+    def _():
+        start(both, (0,))
+        start((tw_sends,), (1, 2))
+        start((pw_sends,), (1, 2))
+
+    upper, lower = pl.ds(0, rows // 2), pl.ds(rows // 2, rows // 2)
+    move_fa = remote(handoff.at[0, upper], arrived.at[upper], move_send.at[0], move_recv.at[0], ahead, f)
+    move_fb = remote(handoff.at[0, lower], arrived.at[lower], move_send.at[1], move_recv.at[1], ahead, f)
+    move_fr = remote(handoff.at[0, lower], relay_h, move_send.at[1], relay_recv.at[0], relay_f_at, f)
+    pass_f = remote(relay_h, arrived.at[lower], relay_send.at[0], move_recv.at[1], relay_f_to, f)
+    move_ba = remote(returning.at[0, upper], back.at[upper], move_send.at[2], move_recv.at[2], behind, f)
+    move_bb = remote(returning.at[0, lower], back.at[lower], move_send.at[3], move_recv.at[3], behind, f)
+    move_br = remote(returning.at[0, lower], relay_r, move_send.at[3], relay_recv.at[1], relay_b_at, f)
+    pass_b = remote(relay_r, back.at[lower], relay_send.at[1], move_recv.at[3], relay_b_to, f)
+
+    @pl.when(near_f)
+    def _():
+        move_fa.start()
+        move_fb.start()
+
+    @pl.when(near_b)
+    def _():
+        move_ba.start()
+        move_bb.start()
+
+    pl.when(far_f)(move_fr.start)
+    pl.when(far_b)(move_br.start)
 
     for padded in (modf, modb, dtp):
         padded[0:cell] = jnp.zeros((cell, ch), BF16)
@@ -178,6 +225,16 @@
         part_out.append(remote(part.at[j], film_in.at[f], part_send.at[d], part_recv.at[d], s, j))
     for copy in part_out:
         copy.start()
+
+    @pl.when(later)
+    def _():
+        start(both, (0,))
+
+    for recvs, sends in ((tw_recvs, tw_sends), (pw_recvs, pw_sends)):
+        recvs[0].wait_recv()
+        pl.when(first)(functools.partial(start, (sends,), (3, 4)))
+    pl.when(far_f)(move_fa.start)
+    pl.when(far_b)(move_ba.start)
     for d in range(1, n_fsdp):
         came = (f + n_fsdp - d) % n_fsdp
         remote(part.at[came], film_in.at[came], part_send.at[d], part_recv.at[d], s, came).wait_recv()
@@ -212,15 +269,12 @@
     loads[2].wait()
     modulate(read_stash, 1, modb)
 
-    @pl.when(jnp.logical_not(first))
+    @pl.when(later)
     def _():
         pl.semaphore_wait(go, 1)
-        ag_begin()
-
-    for recvs, sends in ((tw_recvs, tw_sends), (pw_recvs, pw_sends)):
-        recvs[0].wait_recv()
-        sends[3].start()
-        sends[4].start()
+        for sends in both:
+            start((sends,), (1, 2, 3, 4))
+
     for recvs, sends in ((tw_recvs, tw_sends), (pw_recvs, pw_sends)):
         recvs[1].wait_recv()
         sends[5].start()
@@ -236,6 +290,16 @@
     def _():
         pl.semaphore_signal(go, inc=1, device_id=at(sibling, f), device_id_type=MESH)
 
+    @pl.when(is_relay_f)
+    def _():
+        move_fr.wait_recv()
+        pass_f.start()
+
+    @pl.when(is_relay_b)
+    def _():
+        move_br.wait_recv()
+        pass_b.start()
+
     loads[3].wait()
     loads[4].wait()
 
@@ -256,9 +320,10 @@
     out_b_copy = pltpu.make_async_copy(bout, out_b.at[0], out_sem.at[1])
 
     def forward():
-        move_f.wait_recv()
+        move_fa.wait_recv()
+        move_fb.wait_recv()
         modulate(read_forward, 0, modf)
-        pl.when(is_enc)(gather_end)
+        pl.when(forward_first == 1)(gather_end)
 
         def step(c, carry):
             r0 = pl.multiple_of(c * chunk, chunk)
@@ -277,15 +342,17 @@
 
     half = (tws + pws) // 2
     lo, hi = pl.ds(0, half), pl.ds(half, half)
-    rs_plan = [
-        (grad.at[:, x2, lo], ra_p, fxp, fxm),
-        (grad.at[:, x2, hi], ra_m, fxm, fxp),
-        (grad.at[:, xp, hi], rb_p.at[:, hi], fxp, fxm),
-        (grad.at[:, xm, lo], rb_m.at[:, lo], fxm, fxp),
-        (ra_p, rb_p.at[:, lo], fxp, fxm),
-        (ra_m, rb_m.at[:, hi], fxm, fxp),
-        (zsend, zrecv, fz, fz),
-    ]
+    rs_plan = []
+    for zi in (zo, z):
+        rs_plan += [
+            (grad.at[zi, x2, lo], ra_p.at[zi], fxp, fxm),
+            (grad.at[zi, x2, hi], ra_m.at[zi], fxm, fxp),
+            (grad.at[zi, xp, hi], rb_p.at[zi, hi], fxp, fxm),
+            (grad.at[zi, xm, lo], rb_m.at[zi, lo], fxm, fxp),
+            (ra_p.at[zi], rb_p.at[zi, lo], fxp, fxm),
+            (ra_m.at[zi], rb_m.at[zi, hi], fxm, fxp),
+        ]
+    rs_plan.append((zsend, zrecv, fz, fz))
     rs = [
         remote(src, dst, rs_send.at[k], rs_recv.at[k], s, target)
         for k, (src, dst, target, _) in enumerate(rs_plan)
@@ -296,8 +363,9 @@
     ]
 
     def backward():
-        move_b.wait_recv()
-        pl.when(jnp.logical_not(is_enc))(gather_end)
+        move_ba.wait_recv()
+        move_bb.wait_recv()
+        pl.when(forward_first == 0)(gather_end)
         sums[...] = jnp.zeros_like(sums)
         scale, _ = scale_shift(1)
 
@@ -369,27 +437,27 @@
                     grad[j // RING, j % RING, (b % 3) * block : (b % 3 + 1) * block] = value[
                         i * block : (i + 1) * block
                     ]
-        for k in range(4):
+        for k in (0, 1, 2, 3, 6, 7, 8, 9):
             rs[k].start()
 
     def phase(p, carry):
-        which = p + enc
+        which = p + forward_first
         pl.when(which == 1)(forward)
         pl.when(which != 1)(backward)
         return carry
 
     lax.fori_loop(0, 2, phase, 0)
 
-    def add_rows(dst, src):
-        for zi in range(2):
-            dst[zi] = (dst[zi].astype(F32) + src[zi].astype(F32)).astype(BF16)
-
-    rs[0].wait_recv()
-    add_rows(ra_p, grad.at[:, xp, lo])
-    rs[4].start()
-    rs[1].wait_recv()
-    add_rows(ra_m, grad.at[:, xm, hi])
-    rs[5].start()
+    def add_on(dst, src):
+        dst[...] = (dst[...].astype(F32) + src[...].astype(F32)).astype(BF16)
+
+    for k, zi in ((0, zo), (6, z)):
+        rs[k].wait_recv()
+        add_on(ra_p.at[zi], grad.at[zi, xp, lo])
+        rs[k + 4].start()
+        rs[k + 1].wait_recv()
+        add_on(ra_m.at[zi], grad.at[zi, xm, hi])
+        rs[k + 5].start()
 
     for d in range(1, n_fsdp):
         came = (f + n_fsdp - d) % n_fsdp
@@ -400,18 +468,19 @@
     fg_copy = pltpu.make_async_copy(fg.at[pl.ds(f * fws, fws)], out_fg.at[0], out_sem.at[2])
     fg_copy.start()
 
+    def along_x(zi):
+        return grad[zi, x].astype(F32) + rb_p[zi].astype(F32) + rb_m[zi].astype(F32)
+
     for k in range(2, 6):
         rs[k].wait_recv()
-
-    def along_x(zi):
-        return grad[zi, x].astype(F32) + rb_p[zi].astype(F32) + rb_m[zi].astype(F32)
-
     zsend[...] = along_x(zo).astype(BF16)
-    rs[6].start()
+    rs[12].start()
+    for k in range(8, 12):
+        rs[k].wait_recv()
     own = along_x(z)
     tg[...] = own[0:tws]
     pg[...] = own[tws : tws + pws]
-    rs[6].wait_recv()
+    rs[12].wait_recv()
     tg[...] += zrecv[0:tws].astype(F32)
     pg[...] += zrecv[tws : tws + pws].astype(F32)
     tg_copy = pltpu.make_async_copy(tg, out_tg.at[0], out_sem.at[3])
@@ -419,8 +488,10 @@
     tg_copy.start()
     pg_copy.start()
 
-    for copy in hid_out + part_out + df_out + tw_sends + pw_sends + rs + [move_f, move_b]:
+    for copy in hid_out + part_out + df_out + tw_sends + pw_sends + rs + [move_fa, move_fb, move_ba, move_bb]:
         copy.wait_send()
+    pl.when(is_relay_f)(pass_f.wait_send)
+    pl.when(is_relay_b)(pass_b.wait_send)
 
     def skip_end(c, carry):
         copy = skip_copy(fout, c)
@@ -431,6 +502,30 @@
     lax.fori_loop(0, rows // chunk, skip_end, 0)
     for copy in (out_f_copy, out_b_copy, fg_copy, tg_copy, pg_copy):
         copy.wait()
+
+
+def settle(*refs):
+    sources, results, held, sem_in, sem_out = refs[:6], refs[6:12], refs[12:18], refs[18], refs[19]
+    pieces = []
+    for k in range(6):
+        count = 4 if k < 3 else 1
+        n = sources[k].shape[1] // count
+        pieces += [(k, pl.ds(i * n, n)) for i in range(count)]
+    loads = [
+        pltpu.make_async_copy(sources[k].at[:, piece], held[k].at[:, piece], sem_in.at[i])
+        for i, (k, piece) in enumerate(pieces)
+    ]
+    stores = [
+        pltpu.make_async_copy(held[k].at[:, piece], results[k].at[:, piece], sem_out.at[i])
+        for i, (k, piece) in enumerate(pieces)
+    ]
+    for load in loads:
+        load.start()
+    for load, store in zip(loads, stores):
+        load.wait()
+        store.start()
+    for store in stores:
+        store.wait()
 
 
 def body(
@@ -474,32 +569,43 @@
         vmem(shard), vmem(shard),
         vmem((2, 8, ch), F32), vmem((n_fsdp, 1, 2 * ch), F32),
         vmem((embed, 2 * ch), F32), vmem((tws, ch), F32), vmem((pws, ch), F32),
-        dma((6,)), dma((2,)), dma((2,)), dma((n_fsdp,)), dma((n_fsdp,)), dma((n_fsdp,)), dma((n_fsdp,)),
-        dma((n_fsdp,)), dma((n_fsdp,)), dma((2, 9)), dma((2, 9)), dma((4,)), dma((4,)), dma((7,)), dma((7,)),
-        dma((5,)), pltpu.SemaphoreType.REGULAR,
+        vmem((rows // 2, ch)), vmem((rows // 2, ch)),
+        dma((6,)), dma((4,)), dma((4,)), dma((n_fsdp,)), dma((n_fsdp,)), dma((n_fsdp,)), dma((n_fsdp,)),
+        dma((n_fsdp,)), dma((n_fsdp,)), dma((2, 9)), dma((2, 9)), dma((4,)), dma((4,)), dma((13,)), dma((13,)),
+        dma((5,)), dma((2,)), dma((2,)), pltpu.SemaphoreType.REGULAR,
     ]
     hbm = pl.BlockSpec(memory_space=pl.ANY)
     local = pl.BlockSpec(memory_space=pltpu.VMEM)
     like = jax.ShapeDtypeStruct
+    shapes = (
+        like(handoff.shape, BF16),
+        like(handoff.shape, BF16),
+        like(handoff.shape, BF16),
+        like(temporal_weight.shape, F32),
+        like(point_weight.shape, F32),
+        like(film_weight.shape, F32),
+    )
+    made = pl.pallas_call(
+        functools.partial(tick, sections),
+        out_shape=shapes,
+        in_specs=[local] + [hbm] * 7,
+        out_specs=(hbm,) * 6,
+        scratch_shapes=scratch,
+        compiler_params=pltpu.CompilerParams(
+            collective_id=0, has_side_effects=True, vmem_limit_bytes=56 * 1024 * 1024
+        ),
+        name="relay_tick",
+    )(hid, handoff, returning, stashed_input, skip_held, temporal_weight, point_weight, film_weight)
     return tuple(
         pl.pallas_call(
-            functools.partial(tick, sections),
-            out_shape=(
-                like(handoff.shape, BF16),
-                like(handoff.shape, BF16),
-                like(handoff.shape, BF16),
-                like(temporal_weight.shape, F32),
-                like(point_weight.shape, F32),
-                like(film_weight.shape, F32),
-            ),
-            in_specs=[local] + [hbm] * 7,
+            settle,
+            out_shape=shapes,
+            in_specs=[hbm] * 6,
             out_specs=(hbm,) * 6,
-            scratch_shapes=scratch,
-            compiler_params=pltpu.CompilerParams(
-                collective_id=0, has_side_effects=True, vmem_limit_bytes=56 * 1024 * 1024
-            ),
-            name="relay_tick",
-        )(hid, handoff, returning, stashed_input, skip_held, temporal_weight, point_weight, film_weight)
+            scratch_shapes=[vmem(out.shape, out.dtype) for out in shapes] + [dma((15,)), dma((15,))],
+            compiler_params=pltpu.CompilerParams(vmem_limit_bytes=60 * 1024 * 1024),
+            name="settle",
+        )(*made)
     )
 
 

time: 136 us -> 120 us (0.88)
  the two profiles are of different devices: /device:TPU:2 before, /device:TPU:91 now
where the time goes in v3:
time: 120 us
  Pallas kernels  115 us (96%)
  between operations  2.58 us (2%)
  other arithmetic  1.58 us (1%)
    pallas_call x1, Pallas kernels, body(): pl.pallas_call(functools.partial(tick, sections), out_shape=shapes, in_sp...  111 us
    pallas_call x1, Pallas kernels, body(): pl.pallas_call(settle, out_shape=shapes, in_specs=[hbm] * 6, out_specs=(h...  4.51 us

profile of v3, /device:TPU:91, one launch (start us, length us, event | category | flops | bytes accessed | tf_op | source)
XLA Modules:
  0.0 119.7 jit_solution(6251477762008699206)
XLA Ops:
  2.6 0.1 add_convert_fusion
  2.6 0.8 multiply_reduce_fusion
  3.4 0.1 multiply_sine_fusion
  3.5 0.6 convert_convert_fusion.hid
  4.2 111.0 %relay_tick.1 = (bf16[1,1024,640]{2,1,0:T(8,128)(2,1)}, bf16[1,1024,640]{2,1,0:T(8,128)(2,1)}, bf16[1,1024,640]{2,1,0:T(8,128)(2,1)}, f32[1,240,640]{2,1,0:T(8,1...) custom-call(f32[2,1,256]{2,1,0:T(1,128)} %convert_convert_fusion.hid, bf16[1,1024,640]{2,1,0:T(8,128)(2,1)} %handoff.1, ...), custom_call_target="tpu_custom_call" | custom-call | tf_op jit(solution)/shard_map/relay_tick/pallas_call | solution.py:588
  115.1 4.5 %settle.1 = (bf16[1,1024,640]{2,1,0:T(8,128)(2,1)}, bf16[1,1024,640]{2,1,0:T(8,128)(2,1)}, bf16[1,1024,640]{2,1,0:T(8,128)(2,1)}, f32[1,240,640]{2,1,0:T(8,128)}...) custom-call(bf16[1,1024,640]{2,1,0:T(8,128)(2,1)} %get-tuple-element.12.refs_0_, ...), custom_call_target="tpu_custom_call" | custom-call | tf_op jit(solution)/shard_map/settle/pallas_call | solution.py:600
  (2 shorter events, 0.0 us)

commit v4 on v3

--- a/solution.py
+++ b/solution.py
@@ -55,7 +55,7 @@
 ):
     rows, ch = arrived.shape
     cell = rows // FRAMES
-    chunk = rows // 4
+    chunk = rows // 8
     small = cell
     tws, pws, fws = tw_in.shape[1], pw_in.shape[1], fw_in.shape[1]
     n_fsdp = 2 * RING
@@ -71,7 +71,8 @@
     enc = jnp.where(is_enc, 1, 0)
     first = core == enc
     enc_f = enc.astype(F32)
-    forward_first = enc * jnp.where(first, 1, 0)
+    far_z = jnp.where(z == (s // min(8, sections)) % 2, 0, 1)
+    forward_first = enc * far_z
 
     period = min(8, sections)
     place, run = s % period, s // period
@@ -126,8 +127,6 @@
         remote(hid, hid_all.at[:, f], hid_send.at[d], hid_recv.at[d], s, (f + d) % n_fsdp)
         for d in range(1, n_fsdp)
     ]
-    for copy in hid_out:
-        copy.start()
 
     h0 = {tws: (tws // 2 + 15) // 16 * 16, pws: pws // 2 // 16 * 16}
 
@@ -176,8 +175,10 @@
     @pl.when(first)
     def _():
         start(both, (0,))
-        start((tw_sends,), (1, 2))
-        start((pw_sends,), (1, 2))
+        start(both, (1, 2))
+
+    for copy in hid_out:
+        copy.start()
 
     upper, lower = pl.ds(0, rows // 2), pl.ds(rows // 2, rows // 2)
     move_fa = remote(handoff.at[0, upper], arrived.at[upper], move_send.at[0], move_recv.at[0], ahead, f)
@@ -235,12 +236,6 @@
         pl.when(first)(functools.partial(start, (sends,), (3, 4)))
     pl.when(far_f)(move_fa.start)
     pl.when(far_b)(move_ba.start)
-    for d in range(1, n_fsdp):
-        came = (f + n_fsdp - d) % n_fsdp
-        remote(part.at[came], film_in.at[came], part_send.at[d], part_recv.at[d], s, came).wait_recv()
-    film_in[f] = part[f]
-    film[...] = jnp.sum(film_in[...], axis=0)
-
     def scale_shift(r):
         return 1.0 + film[r, :, 0:ch], film[r, :, ch : 2 * ch]
 
@@ -265,12 +260,19 @@
     def read_grad(r0, n):
         return back[pl.ds(r0, n)].astype(F32) + held_v[pl.ds(r0, n)].astype(F32) * enc_f
 
-    loads[1].wait()
-    loads[2].wait()
-    modulate(read_stash, 1, modb)
+    def settle_film():
+        for d in range(1, n_fsdp):
+            came = (f + n_fsdp - d) % n_fsdp
+            remote(part.at[came], film_in.at[came], part_send.at[d], part_recv.at[d], s, came).wait_recv()
+        film_in[f] = part[f]
+        film[...] = jnp.sum(film_in[...], axis=0)
+        loads[1].wait()
+        loads[2].wait()
+        modulate(read_stash, 1, modb)
 
     @pl.when(later)
     def _():
+        settle_film()
         pl.semaphore_wait(go, 1)
         for sends in both:
             start((sends,), (1, 2, 3, 4))
@@ -280,6 +282,16 @@
         sends[5].start()
         recvs[2].wait_recv()
         sends[6].start()
+    @pl.when(is_relay_f)
+    def _():
+        move_fr.wait_recv()
+        pass_f.start()
+
+    @pl.when(is_relay_b)
+    def _():
+        move_br.wait_recv()
+        pass_b.start()
+
     for recvs, sends in ((tw_recvs, tw_sends), (pw_recvs, pw_sends)):
         recvs[3].wait_recv()
         sends[7].start()
@@ -289,24 +301,14 @@
     @pl.when(first)
     def _():
         pl.semaphore_signal(go, inc=1, device_id=at(sibling, f), device_id_type=MESH)
-
-    @pl.when(is_relay_f)
-    def _():
-        move_fr.wait_recv()
-        pass_f.start()
-
-    @pl.when(is_relay_b)
-    def _():
-        move_br.wait_recv()
-        pass_b.start()
+        settle_film()
 
     loads[3].wait()
     loads[4].wait()
 
-    def gather_end():
-        for recvs in (tw_recvs, pw_recvs):
-            for k in range(5, 9):
-                recvs[k].wait_recv()
+    def gather_end(recvs):
+        for k in range(5, 9):
+            recvs[k].wait_recv()
 
     def skip_copy(src, c):
         piece = pl.ds(pl.multiple_of(c * chunk, chunk), chunk)
@@ -323,12 +325,13 @@
         move_fa.wait_recv()
         move_fb.wait_recv()
         modulate(read_forward, 0, modf)
-        pl.when(forward_first == 1)(gather_end)
+        pl.when(forward_first == 1)(functools.partial(gather_end, tw_recvs))
 
         def step(c, carry):
             r0 = pl.multiple_of(c * chunk, chunk)
             t = temporal_of(modf, r0)
             gate = (t * sigmoid(t)).astype(BF16)
+            pl.when(jnp.logical_and(c == 0, forward_first == 1))(functools.partial(gather_end, pw_recvs))
             fout[pl.ds(r0, chunk)] = (read_forward(r0, chunk) + dot(gate, pw[...])).astype(BF16)
 
             @pl.when(is_enc)
@@ -365,7 +368,7 @@
     def backward():
         move_ba.wait_recv()
         move_bb.wait_recv()
-        pl.when(forward_first == 0)(gather_end)
+        pl.when(forward_first == 0)(functools.partial(gather_end, tw_recvs))
         sums[...] = jnp.zeros_like(sums)
         scale, _ = scale_shift(1)
 
@@ -378,6 +381,7 @@
                 gated[pl.ds(r0, chunk)] = (t * sig).astype(BF16)
                 g = read_grad(r0, chunk).astype(BF16)
                 gb[pl.ds(r0, chunk)] = g
+                pl.when(jnp.logical_and(c == 0, forward_first == 0))(functools.partial(gather_end, pw_recvs))
                 dgate = nt(g, pw[...]).astype(BF16).astype(F32)
                 dtp[pl.ds(pl.multiple_of(r0 + cell, cell), chunk)] = (
                     dgate * (sig * (1.0 + t * (1.0 - sig)))
@@ -571,7 +575,7 @@
         vmem((embed, 2 * ch), F32), vmem((tws, ch), F32), vmem((pws, ch), F32),
         vmem((rows // 2, ch)), vmem((rows // 2, ch)),
         dma((6,)), dma((4,)), dma((4,)), dma((n_fsdp,)), dma((n_fsdp,)), dma((n_fsdp,)), dma((n_fsdp,)),
-        dma((n_fsdp,)), dma((n_fsdp,)), dma((2, 9)), dma((2, 9)), dma((4,)), dma((4,)), dma((13,)), dma((13,)),
+        dma((n_fsdp,)), dma((n_fsdp,)), dma((2, 9)), dma((2, 9)), dma((8,)), dma((8,)), dma((13,)), dma((13,)),
         dma((5,)), dma((2,)), dma((2,)), pltpu.SemaphoreType.REGULAR,
     ]
     hbm = pl.BlockSpec(memory_space=pl.ANY)

time: 120 us -> 116 us (0.967)
  the two profiles are of different devices: /device:TPU:91 before, /device:TPU:57 now
where the time goes in v4:
time: 116 us
  Pallas kernels  112 us (97%)
  between operations  2.58 us (2%)
  other arithmetic  1.58 us (1%)
    pallas_call x1, Pallas kernels, body(): pl.pallas_call(functools.partial(tick, sections), out_shape=shapes, in_sp...  107 us
    pallas_call x1, Pallas kernels, body(): pl.pallas_call(settle, out_shape=shapes, in_specs=[hbm] * 6, out_specs=(h...  4.51 us

profile of v4, /device:TPU:57, one launch (start us, length us, event | category | flops | bytes accessed | tf_op | source)
XLA Modules:
  0.0 115.8 jit_solution(13644047690167425691)
XLA Ops:
  2.6 0.1 add_convert_fusion
  2.6 0.8 multiply_reduce_fusion
  3.4 0.1 multiply_sine_fusion
  3.5 0.6 convert_convert_fusion.hid
  4.2 107.1 %relay_tick.1 = (bf16[1,1024,640]{2,1,0:T(8,128)(2,1)}, bf16[1,1024,640]{2,1,0:T(8,128)(2,1)}, bf16[1,1024,640]{2,1,0:T(8,128)(2,1)}, f32[1,240,640]{2,1,0:T(8,1...) custom-call(f32[2,1,256]{2,1,0:T(1,128)} %convert_convert_fusion.hid, bf16[1,1024,640]{2,1,0:T(8,128)(2,1)} %handoff.1, ...), custom_call_target="tpu_custom_call" | custom-call | tf_op jit(solution)/shard_map/relay_tick/pallas_call | solution.py:592
  111.3 4.5 %settle.1 = (bf16[1,1024,640]{2,1,0:T(8,128)(2,1)}, bf16[1,1024,640]{2,1,0:T(8,128)(2,1)}, bf16[1,1024,640]{2,1,0:T(8,128)(2,1)}, f32[1,240,640]{2,1,0:T(8,128)}...) custom-call(bf16[1,1024,640]{2,1,0:T(8,128)(2,1)} %get-tuple-element.12.refs_0_, ...), custom_call_target="tpu_custom_call" | custom-call | tf_op jit(solution)/shard_map/settle/pallas_call | solution.py:604
  (2 shorter events, 0.0 us)

commit v5 on v4

--- a/solution.py
+++ b/solution.py
@@ -72,7 +72,7 @@
     first = core == enc
     enc_f = enc.astype(F32)
     far_z = jnp.where(z == (s // min(8, sections)) % 2, 0, 1)
-    forward_first = enc * far_z
+    forward_first = enc * far_z * jnp.where(first, 1, 0)
 
     period = min(8, sections)
     place, run = s % period, s // period

time: 116 us -> 119 us (1.026)
  the two profiles are of different devices: /device:TPU:57 before, /device:TPU:217 now
where the time goes in v5:
time: 119 us
  Pallas kernels  115 us (97%)
  between operations  2.58 us (2%)
  other arithmetic  1.58 us (1%)
    pallas_call x1, Pallas kernels, body(): pl.pallas_call(functools.partial(tick, sections), out_shape=shapes, in_sp...  110 us
    pallas_call x1, Pallas kernels, body(): pl.pallas_call(settle, out_shape=shapes, in_specs=[hbm] * 6, out_specs=(h...  4.51 us

profile of v5, /device:TPU:217, one launch (start us, length us, event | category | flops | bytes accessed | tf_op | source)
XLA Modules:
  0.0 119.1 jit_solution(3170399850915080432)
XLA Ops:
  2.6 0.1 add_convert_fusion
  2.6 0.8 multiply_reduce_fusion
  3.4 0.1 multiply_sine_fusion
  3.5 0.6 convert_convert_fusion.hid
  4.2 110.5 %relay_tick.1 = (bf16[1,1024,640]{2,1,0:T(8,128)(2,1)}, bf16[1,1024,640]{2,1,0:T(8,128)(2,1)}, bf16[1,1024,640]{2,1,0:T(8,128)(2,1)}, f32[1,240,640]{2,1,0:T(8,1...) custom-call(f32[2,1,256]{2,1,0:T(1,128)} %convert_convert_fusion.hid, bf16[1,1024,640]{2,1,0:T(8,128)(2,1)} %handoff.1, ...), custom_call_target="tpu_custom_call" | custom-call | tf_op jit(solution)/shard_map/relay_tick/pallas_call | solution.py:592
  114.6 4.5 %settle.1 = (bf16[1,1024,640]{2,1,0:T(8,128)(2,1)}, bf16[1,1024,640]{2,1,0:T(8,128)(2,1)}, bf16[1,1024,640]{2,1,0:T(8,128)(2,1)}, f32[1,240,640]{2,1,0:T(8,128)}...) custom-call(bf16[1,1024,640]{2,1,0:T(8,128)(2,1)} %get-tuple-element.12.refs_0_, ...), custom_call_target="tpu_custom_call" | custom-call | tf_op jit(solution)/shard_map/settle/pallas_call | solution.py:604
  (2 shorter events, 0.0 us)
